TPU v7x, 768 devices: a whole 4x8x12 slice. The times are simulated.
768 devices in a mesh: dp: 128 (over z_hi, y, x), tensor: 6 (over z_lo, core).
Axes of the slice: x: 4, y: 8, z: 12 (z_hi: 4, z_lo: 3; z = z_hi * 3 + z_lo), core: 2. Of those that a mesh axis runs over, the one named last changes fastest.
Arguments:
- grad: bfloat16 [4096, 12288], P('dp', 'tensor'), may hold values from -48 to 48
- second_moment: float32 [4096, 12288], P('dp', 'tensor'), may hold values from 0.05 to 5
- left_roots: bfloat16 [4, 1024, 1024], P(None, 'dp'), may hold values from -5 to 5
- right_roots: bfloat16 [12, 1024, 1024], P('tensor'), may hold values from -5 to 5
Outputs:
- update: bfloat16 [4096, 12288], P('dp', 'tensor')
- moment_next: float32 [4096, 12288], P('dp', 'tensor')
All inputs are finite; a program needn't handle non-finite values.
Results may differ from a plain program's by a relative error of at most 0.0059.
Values may be sent and summed in bfloat16 or wider, within the bound.
No kernel may reach another device: no remote copies, remote signals or barrier semaphores. Data moves between devices by JAX's collectives and lax.ppermute only.
A program may use at most 32 MiB of HBM per device.

v0:
```python
import jax
import jax.numpy as jnp
from jax import lax
from jax.sharding import PartitionSpec as P


def block_partial(field, rows, col_blocks, blk, picker):
    shaped = field.reshape(rows, col_blocks, blk)
    partial_sum = jnp.sum(shaped * shaped, axis=(0, 2))
    return picker[:, None] * partial_sum[None, :]


def on_device(grad, second_moment, left_roots, right_roots):
    rows, width = grad.shape
    col_blocks, blk = (right_roots.shape[0], right_roots.shape[1])
    row_blocks = left_roots.shape[0]
    n_data = lax.axis_size("dp")
    cols = width // n_data
    wide = grad.astype(jnp.float32)
    moment_next = 0.95 * second_moment + 0.05 * wide * wide
    adam = wide / (jnp.sqrt(moment_next) + 1e-08)
    position = lax.axis_index("dp")
    row_block = position * rows // blk
    picker = (lax.iota(jnp.int32, row_blocks) == row_block).astype(jnp.float32)
    adam_part = block_partial(adam, rows, col_blocks, blk, picker)
    adam_sq = lax.psum(adam_part, "dp")
    projected = jnp.einsum(
        "icj,cjk->ick",
        grad.reshape(rows, col_blocks, blk),
        right_roots,
        preferred_element_type=jnp.float32,
    ).astype(jnp.bfloat16)
    pieces = projected.reshape(rows, n_data, cols).transpose(1, 2, 0)
    columns = lax.all_to_all(pieces, "dp", split_axis=0, concat_axis=2, tiled=True)
    tall = columns.reshape(cols, row_blocks, blk)
    full_roots = lax.all_gather(left_roots, "dp", axis=1, tiled=True)
    mixed = jnp.einsum("crj,rij->cri", tall, full_roots, preferred_element_type=jnp.float32)
    mixed_half = mixed.astype(jnp.bfloat16).reshape(cols, n_data, rows)
    returned = lax.all_to_all(mixed_half, "dp", split_axis=1, concat_axis=0, tiled=True)
    result = returned.reshape(width, rows).T.astype(jnp.float32)
    mixed_part = block_partial(result, rows, col_blocks, blk, picker)
    mixed_sq = lax.psum(mixed_part, "dp")
    factor = jnp.sqrt(adam_sq) / (jnp.sqrt(mixed_sq) + 1e-06)
    chosen = jnp.sum(picker[:, None] * factor, axis=0)
    scaled = result.reshape(rows, col_blocks, blk) * chosen[None, :, None]
    update = scaled.reshape(rows, width).astype(jnp.bfloat16)
    return (update, moment_next)


def solution(mesh):
    return jax.shard_map(
        on_device,
        mesh=mesh,
        in_specs=(
            P("dp", "tensor"),
            P("dp", "tensor"),
            P(None, "dp", None),
            P("tensor", None, None),
        ),
        out_specs=(P("dp", "tensor"), P("dp", "tensor")),
        check_vma=False,
    )
```

profile of v0, /device:TPU:2, one launch (start us, length us, event | category | flops | bytes accessed | tf_op | source)
XLA Modules:
  0.0 665.7 jit_solution(13369998663286251614)
XLA Ops:
  7.2 0.0 all-gather.2.cloned.1.call-start
  7.2 0.7 all-gather.2.cloned.1.call-update
  7.9 3.1 fusion.1
  11.0 0.0 copy-start
  11.0 0.0 copy-start.1
  11.0 0.3 copy.22
  11.3 0.3 reshape.44
  11.6 40.8 %all_to_all.24 = bf16[128,2,256]{2,1,0:T(2,128)(2,1)S(1)} all-to-all(bf16[128,2,256]{2,1,0:T(2,128)(2,1)S(1)} %reshape.44), channel_id=1, replica_groups=mesh['dp'=128,'tensor'=6] {'dp'}, dimensions={0} | all-to-all | bytes 262144 | tf_op jit(solution)/shard_map/all_to_all | solution.py:34
  52.5 0.3 reshape.45
  52.7 0.1 copy.23
  52.9 0.5 reshape.40
  53.4 152.5 %all-gather.2.cloned.1.call-done = bf16[4,1024,1024]{2,1,0:T(8,128)(2,1)} async-done(((bf16[4,8,1024]{2,1,0:T(8,128)(2,1)}), bf16[4,1024,1024]{2,1,0:T(8,128)(2,1)}) %all-gather.2.cloned.1.call-update) | async-done | bytes 8388624 | tf_op jit(solution)/shard_map/all_gather | solution.py:36
  205.9 5.6 fusion
  211.5 0.1 copy.25
  211.7 0.3 reshape.41
  212.0 0.3 copy.39
  212.3 1.0 reshape.46
  213.3 26.5 %all-to-all-start.1 = ((bf16[128,2,256]{2,1,0:T(2,128)(2,1)}), bf16[128,2,256]{2,1,0:T(2,128)(2,1)S(1)}, u32[]{:S(2)}, u32[]{:S(2)}) async-start(bf16[128,2,256]{2,1,0:T(2,128)(2,1)} %reshape.46), calls=%async_computation.1 | async-start | bytes 262144 | tf_op jit(solution)/shard_map/all_to_all | solution.py:39
  239.9 0.0 copy-done
  239.9 0.0 copy-done.1
  239.9 0.8 fusion.6
  240.7 0.1 reduce_sum.36
  240.9 14.6 %all-to-all-done.1 = bf16[128,2,256]{2,1,0:T(2,128)(2,1)S(1)} async-done(((bf16[128,2,256]{2,1,0:T(2,128)(2,1)}), bf16[128,2,256]{2,1,0:T(2,128)(2,1)S(1)}, u32[]{:S(2)}, u32[]{:S(2)}) %all-to-all-start.1) | async-done | bytes 131104 | tf_op jit(solution)/shard_map/all_to_all | solution.py:39
  255.5 0.3 reshape.47
  255.8 0.3 fusion.2
  256.1 0.1 reduce_sum.46
  256.3 0.1 broadcast_multiply_fusion.1
  256.3 401.1 %all-reduce = (f32[4,2]{0,1:T(2,128)S(1)}, f32[4,2]{0,1:T(2,128)S(1)}) all-reduce(f32[4,2]{0,1:T(2,128)S(1)} %get-tuple-element.13, f32[4,2]{0,1:T(2,128)S(1)} %get-tuple-element.12), channel_id=1, replica_groups=mesh['dp'=128,'tensor'=6] {'dp'}, use_global_device_ids=true, to_apply=%region_5.6 | all-reduce | flops 16 | bytes 128 | tf_op jit(solution)/shard_map/psum | solution.py:42
  657.5 0.1 multiply_reduce_fusion
  657.6 0.1 broadcast_bitcast_fusion
  657.7 0.3 fusion.3
  658.0 0.8 copy.27
  (4 shorter events, 0.0 us)
Async XLA Ops:
  7.2 198.7 %all-gather.2.cloned.1.call-start = ((), (), s32[]{:S(2)}) async-start(), calls=%async_computation.2 | async-start | bytes 8454144 | tf_op jit(solution)/shard_map/all_gather | solution.py:36
  11.0 228.9 %copy-start = (bf16[32,2048]{1,0:T(8,128)(2,1)S(1)}, bf16[32,2048]{1,0:T(8,128)(2,1)}, u32[]{:S(2)}) copy-start(bf16[32,2048]{1,0:T(8,128)(2,1)} %param.4) | copy-start | bytes 393220
  11.0 228.9 %copy-start.1 = (f32[32,2048]{1,0:T(8,128)S(1)}, f32[32,2048]{1,0:T(8,128)}, u32[]{:S(2)}) copy-start(f32[32,2048]{1,0:T(8,128)} %param.5) | copy-start | bytes 786436
  213.3 42.2 %all-to-all-start.1 = ((bf16[128,2,256]{2,1,0:T(2,128)(2,1)}), bf16[128,2,256]{2,1,0:T(2,128)(2,1)S(1)}, u32[]{:S(2)}, u32[]{:S(2)}) async-start(bf16[128,2,256]{2,1,0:T(2,128)(2,1)} %reshape.46), calls=%async_computation.1 | async-start | bytes 262144 | tf_op jit(solution)/shard_map/all_to_all | solution.py:39
Sparse Core Ops, SparseCore 0:
  13.3 192.5 all-gather.1
where the time goes:
time: 666 us
  blocking collectives  442 us (66%)
  waiting for transfers between devices  168 us (25%)
  starting transfers between devices  26.6 us (4%)
  between operations  14.2 us (2%)
  matrix products  8.74 us (1%)
    psum x1, blocking collectives, on_device(): mixed_sq = lax.psum(mixed_part, 'dp')  401 us
    all_gather x1, waiting for transfers between devices, on_device(): full_roots = lax.all_gather(left_roots, 'dp', axis=1, tiled=True)  152 us
    all_to_all x1, blocking collectives, on_device(): lax.all_to_all(pieces, 'dp', split_axis=0, concat_axis=2, tiled=True)  40.8 us
    all_to_all x1, starting transfers between devices, on_device(): lax.all_to_all(mixed_half, 'dp', split_axis=1, concat_axis=0, tiled=True)  26.5 us
    all_to_all x1, waiting for transfers between devices, on_device(): lax.all_to_all(mixed_half, 'dp', split_axis=1, concat_axis=0, tiled=True)  14.6 us
  transfers between devices with their start and end apart: 2, of which 2 were waited for; matrix products, arithmetic and copies ran while one was open for 1% of the time, Pallas kernels for 0%

commit v1 on v0

v1 whole, which is shorter than its diff:
```python
import jax
import jax.numpy as jnp
from jax import lax
from jax.sharding import Mesh, PartitionSpec as P

ZH, YY, XX = 4, 8, 4
PLANE = ("y", "x")
COLUMN = ("zh", "y")


def split3(value):
    high = lax.reduce_precision(value, 8, 7)
    rest = value - high
    middle = lax.reduce_precision(rest, 8, 7)
    return jnp.stack([high, middle, rest - middle], axis=-1)


def on_device(grad, second_moment, left_roots, right_roots):
    rows, width = grad.shape
    col_blocks, blk = right_roots.shape[:2]
    peers = YY * XX
    cols = width // YY
    sub = rows // XX
    send = jnp.broadcast_to(left_roots[:, None], (ZH, YY) + left_roots.shape[1:])
    send = send.reshape((ZH * YY,) + left_roots.shape[1:])
    left = lax.all_to_all(send, COLUMN, 0, 0, tiled=True).reshape(-1, blk)

    wide = grad.astype(jnp.float32)
    moment_next = 0.95 * second_moment + 0.05 * wide * wide
    adam = wide / (jnp.sqrt(moment_next) + 1e-08)
    adam_part = jnp.sum((adam * adam).reshape(rows, col_blocks, blk), axis=(0, 2))

    projected = jnp.concatenate(
        [
            jnp.dot(
                grad[:, c * blk : (c + 1) * blk],
                right_roots[c],
                preferred_element_type=jnp.float32,
            ).astype(jnp.bfloat16)
            for c in range(col_blocks)
        ],
        axis=1,
    )
    pieces = projected.reshape(rows, YY, cols).transpose(1, 0, 2)
    pieces = jnp.broadcast_to(pieces[:, None], (YY, XX, rows, cols))
    pieces = pieces.reshape(peers, rows, cols)
    tall = lax.all_to_all(pieces, PLANE, 0, 0, tiled=True).reshape(peers * rows, cols)

    mixed = jnp.dot(left, tall, preferred_element_type=jnp.float32).astype(jnp.bfloat16)
    again = mixed.astype(jnp.float32)
    mixed_part = jnp.sum(again * again)
    sums = split3(jnp.concatenate([mixed_part[None], adam_part])).reshape(-1)
    extra = jnp.zeros((8, 128), jnp.float32).at[0, : sums.shape[0]].set(sums)
    extra = jnp.broadcast_to(extra.astype(jnp.bfloat16), (peers, 8, 128))
    out = mixed.reshape(peers, sub, cols // 128, 128).transpose(0, 2, 1, 3)
    out = out.reshape(peers, -1, 128)
    n_out = out.shape[1]
    back = lax.all_to_all(jnp.concatenate([out, extra], axis=1), PLANE, 0, 0, tiled=True)

    sums = back[:, n_out, : 3 * (1 + col_blocks)].astype(jnp.float32)
    sums = sums.reshape(col_blocks, peers // col_blocks, 1 + col_blocks, 3).sum(axis=3)
    mixed_sq = jnp.sum(sums[:, :, 0], axis=1)
    adam_sq = jnp.sum(sums[:, :, 1:], axis=(0, 1))
    factor = jnp.sqrt(adam_sq) / (jnp.sqrt(mixed_sq) + 1e-06)
    result = back[:, :n_out].reshape(YY, XX, cols // 128, sub, 128)
    result = result.transpose(1, 3, 0, 2, 4).astype(jnp.float32)
    scaled = result * jnp.repeat(factor, YY // col_blocks)[None, None, :, None, None]
    update = scaled.astype(jnp.bfloat16).reshape(rows, width)
    return (update, moment_next)


def solution(mesh):
    tensor = mesh.shape["tensor"]
    fine = Mesh(mesh.devices.reshape(ZH, YY, XX, tensor), ("zh", "y", "x", "tensor"))
    dp = ("zh", "y", "x")
    return jax.shard_map(
        on_device,
        mesh=fine,
        in_specs=(
            P(dp, "tensor"),
            P(dp, "tensor"),
            P(None, dp, None),
            P("tensor", None, None),
        ),
        out_specs=(P(dp, "tensor"), P(dp, "tensor")),
        check_vma=False,
    )
```

time: 666 us -> 95.3 us (0.14)
  the two profiles are of different devices: /device:TPU:2 before, /device:TPU:64 now
where the time goes in v1:
time: 95.3 us; the launch traced here: 95 us
  blocking collectives  45.4 us (48%)
  waiting for transfers between devices  23.6 us (25%)
  starting transfers between devices  15.4 us (16%)
  matrix products  5.19 us (5%)
  local copies, waits for them, and re-layouts  2.49 us (3%)
  other arithmetic  2.1 us (2%)
    all_to_all x1, blocking collectives, on_device(): lax.all_to_all(pieces, PLANE, 0, 0, tiled=True).reshape(peers * rows, cols)  27.5 us
    all_to_all x1, waiting for transfers between devices, on_device(): left = lax.all_to_all(send, COLUMN, 0, 0, tiled=True).reshape(-1, blk)  23.6 us
    all_to_all x1, blocking collectives, on_device(): lax.all_to_all(jnp.concatenate([out, extra], axis=1), PLANE, 0, 0, tiled=...  17.9 us
    all_to_all x1, starting transfers between devices, on_device(): left = lax.all_to_all(send, COLUMN, 0, 0, tiled=True).reshape(-1, blk)  15.4 us
    dot_general x2, matrix products, on_device(): jnp.dot(grad[:, c * blk:(c + 1) * blk], right_roots[c], preferred_element...  4.24 us
  transfers between devices with their start and end apart: 1, of which 1 were waited for; matrix products, arithmetic and copies ran while one was open for 1% of the time, Pallas kernels for 0%

profile of v1, /device:TPU:64, one launch (start us, length us, event | category | flops | bytes accessed | tf_op | source)
XLA Modules:
  0.0 95.0 jit_solution(9518843914067508728)
XLA Ops:
  0.6 0.0 copy-start.1
  0.6 0.0 copy-start.2
  0.7 0.0 copy-start
  0.7 2.1 %fusion.10 = bf16[32,1024]{1,0:T(8,128)(2,1)S(1)} fusion(bf16[2,1024,1024]{2,1,0:T(8,128)(2,1)} %param.9, bf16[32,2048]{1,0:T(8,128)(2,1)} %param.6), kind=kOutput, calls=%fused_computation.9 | convolution fusion | flops 67141632 | bytes 2228224 | tf_op jit(solution)/shard_map/dot_general | solution.py:35
  2.8 2.1 %fusion.7 = bf16[32,1024]{1,0:T(8,128)(2,1)S(1)} fusion(bf16[2,1024,1024]{2,1,0:T(8,128)(2,1)} %param.9, bf16[32,2048]{1,0:T(8,128)(2,1)} %param.6), kind=kOutput, calls=%fused_computation.8 | convolution fusion | flops 67141632 | bytes 2228224 | tf_op jit(solution)/shard_map/dot_general | solution.py:35
  5.0 0.1 broadcast_in_dim.8
  5.1 27.5 %all_to_all.15 = bf16[32,32,256]{2,1,0:T(8,128)(2,1)S(1)} all-to-all(bf16[32,32,256]{2,1,0:T(8,128)(2,1)S(1)} %bitcast.38), channel_id=1, replica_groups=mesh['zh'=4,'y'=8,'x'=4,'tensor'=6] {'y','x'}, dimensions={0} | all-to-all | bytes 1048576 | tf_op jit(solution)/shard_map/all_to_all | solution.py:47
  32.5 0.0 copy-done.2
  32.5 0.8 broadcast_in_dim.9
  33.4 15.4 %all-to-all-start.1 = ((bf16[32,8,1024]{2,1,0:T(8,128)(2,1)}), bf16[32,8,1024]{2,1,0:T(8,128)(2,1)S(1)}, u32[]{:S(2)}, u32[]{:S(2)}) async-start(bf16[32,8,1024]{2,1,0:T(8,128)(2,1)} %bitcast.5), calls=%async_computation.1 | async-start | bytes 1048576 | tf_op jit(solution)/shard_map/all_to_all | solution.py:26
  48.8 0.0 copy-done.1
  48.8 0.0 copy-done
  48.8 0.8 fusion.17
  49.7 0.1 reduce_sum.55
  49.8 23.6 %all-to-all-done.1 = bf16[32,8,1024]{2,1,0:T(8,128)(2,1)S(1)} async-done(((bf16[32,8,1024]{2,1,0:T(8,128)(2,1)}), bf16[32,8,1024]{2,1,0:T(8,128)(2,1)S(1)}, u32[]{:S(2)}, u32[]{:S(2)}) %all-to-all-start.1) | async-done | bytes 524320 | tf_op jit(solution)/shard_map/all_to_all | solution.py:26
  73.4 1.0 %multiply_reduce_fusion = (f32[]{:T(128)}, bf16[256,256]{0,1:T(8,128)(2,1)S(1)}) fusion(bf16[1024,256]{1,0:T(8,128)(2,1)S(1)} %bitcast.40, bf16[32,8,1024]{2,1,0:T(8,128)(2,1)S(1)} %all-to-all-done.1), kind=kOutput, calls=%fused_computation.17 | convolution fusion | flops 134479872 | bytes 1179652 | tf_op jit(solution)/shard_map/dot_general | solution.py:49
  74.4 0.7 reduce-precision_convert_fusion.1
  75.1 0.1 copy.36
  75.2 0.1 reshape.177
  75.3 0.1 copy.35
  75.5 17.9 %all_to_all.16 = bf16[32,24,128]{2,1,0:T(8,128)(2,1)S(1)} all-to-all(bf16[32,24,128]{2,1,0:T(8,128)(2,1)S(1)} %pad_maximum_fusion), channel_id=1, replica_groups=mesh['zh'=4,'y'=8,'x'=4,'tensor'=6] {'y','x'}, dimensions={0} | all-to-all | bytes 393216 | tf_op jit(solution)/shard_map/all_to_all | solution.py:58
  93.4 0.1 copy.39
  93.5 0.1 reshape.180
  93.6 0.1 slice_reduce_fusion
  93.7 0.1 slice_reduce_fusion.1
  93.9 0.1 broadcast_in_dim.11
  93.9 0.1 mul.39
  94.0 0.1 fusion.18
  94.1 0.1 copy.38
  94.3 0.7 reshape.178
  (14 shorter events, 0.2 us)
Async XLA Ops:
  0.6 48.2 %copy-start.1 = (bf16[32,2048]{1,0:T(8,128)(2,1)S(1)}, bf16[32,2048]{1,0:T(8,128)(2,1)}, u32[]{:S(2)}) copy-start(bf16[32,2048]{1,0:T(8,128)(2,1)} %param.6) | copy-start | bytes 393220
  0.6 31.9 %copy-start.2 = (bf16[4,8,1024]{2,1,0:T(8,128)(2,1)S(1)}, bf16[4,8,1024]{2,1,0:T(8,128)(2,1)}, u32[]{:S(2)}) copy-start(bf16[4,8,1024]{2,1,0:T(8,128)(2,1)} %param.8) | copy-start | bytes 196612
  0.7 48.2 %copy-start = (f32[32,2048]{1,0:T(8,128)S(1)}, f32[32,2048]{1,0:T(8,128)}, u32[]{:S(2)}) copy-start(f32[32,2048]{1,0:T(8,128)} %param.7) | copy-start | bytes 786436
  33.4 40.1 %all-to-all-start.1 = ((bf16[32,8,1024]{2,1,0:T(8,128)(2,1)}), bf16[32,8,1024]{2,1,0:T(8,128)(2,1)S(1)}, u32[]{:S(2)}, u32[]{:S(2)}) async-start(bf16[32,8,1024]{2,1,0:T(8,128)(2,1)} %bitcast.5), calls=%async_computation.1 | async-start | bytes 1048576 | tf_op jit(solution)/shard_map/all_to_all | solution.py:26

commit v2 on v1

--- a/solution.py
+++ b/solution.py
@@ -5,7 +5,6 @@
 
 ZH, YY, XX = 4, 8, 4
 PLANE = ("y", "x")
-COLUMN = ("zh", "y")
 
 
 def split3(value):
@@ -21,9 +20,11 @@
     peers = YY * XX
     cols = width // YY
     sub = rows // XX
-    send = jnp.broadcast_to(left_roots[:, None], (ZH, YY) + left_roots.shape[1:])
-    send = send.reshape((ZH * YY,) + left_roots.shape[1:])
-    left = lax.all_to_all(send, COLUMN, 0, 0, tiled=True).reshape(-1, blk)
+    core = lax.axis_index("core")
+    half = blk // 2
+    mine = lax.dynamic_slice_in_dim(left_roots, core * half, half, axis=2)
+    mine = lax.all_to_all(mine, "zh", 0, 0, tiled=True)
+    n_left = ZH * mine.shape[1] * half // cols
 
     wide = grad.astype(jnp.float32)
     moment_next = 0.95 * second_moment + 0.05 * wide * wide
@@ -42,9 +43,18 @@
         axis=1,
     )
     pieces = projected.reshape(rows, YY, cols).transpose(1, 0, 2)
-    pieces = jnp.broadcast_to(pieces[:, None], (YY, XX, rows, cols))
-    pieces = pieces.reshape(peers, rows, cols)
-    tall = lax.all_to_all(pieces, PLANE, 0, 0, tiled=True).reshape(peers * rows, cols)
+    packed = mine.reshape(ZH, -1, half // cols, cols).transpose(0, 2, 1, 3)
+    packed = jnp.broadcast_to(packed.reshape(1, n_left, cols), (YY, n_left, cols))
+    got = lax.all_to_all(jnp.concatenate([pieces, packed], axis=1), "y", 0, 0, tiled=True)
+    own = got[:, rows:]
+    other = lax.ppermute(own, "core", [(0, 1), (1, 0)])
+    strip = jnp.broadcast_to(got[None, :, :rows], (XX, YY, rows, cols))
+    strip = lax.all_to_all(strip, "x", 0, 0, tiled=True)
+    tall = strip.transpose(1, 0, 2, 3).reshape(peers * rows, cols)
+    first = jnp.where(core == 0, own, other)
+    second = jnp.where(core == 0, other, own)
+    left = jnp.stack([first, second], axis=0).reshape(2, YY, ZH, half // cols, -1, cols)
+    left = left.transpose(2, 1, 4, 0, 3, 5).reshape(-1, blk)
 
     mixed = jnp.dot(left, tall, preferred_element_type=jnp.float32).astype(jnp.bfloat16)
     again = mixed.astype(jnp.float32)
@@ -71,17 +81,19 @@
 
 def solution(mesh):
     tensor = mesh.shape["tensor"]
-    fine = Mesh(mesh.devices.reshape(ZH, YY, XX, tensor), ("zh", "y", "x", "tensor"))
-    dp = ("zh", "y", "x")
+    cores = 2 if tensor % 2 == 0 else 1
+    names = ("zh", "y", "x", "zl", "core")
+    fine = Mesh(mesh.devices.reshape(ZH, YY, XX, tensor // cores, cores), names)
+    dp, columns = ("zh", "y", "x"), ("zl", "core")
     return jax.shard_map(
         on_device,
         mesh=fine,
         in_specs=(
-            P(dp, "tensor"),
-            P(dp, "tensor"),
+            P(dp, columns),
+            P(dp, columns),
             P(None, dp, None),
-            P("tensor", None, None),
+            P(columns, None, None),
         ),
-        out_specs=(P(dp, "tensor"), P(dp, "tensor")),
+        out_specs=(P(dp, columns), P(dp, columns)),
         check_vma=False,
     )

time: 95.3 us -> 82.2 us (0.86)
  the two profiles are of different devices: /device:TPU:64 before, /device:TPU:8 now
where the time goes in v2:
time: 82.2 us; the launch traced here: 81.8 us
  blocking collectives  34 us (41%)
  starting transfers between devices  20.7 us (25%)
  waiting for transfers between devices  14.1 us (17%)
  matrix products  5.15 us (6%)
  local copies, waits for them, and re-layouts  4.76 us (6%)
  other arithmetic  2.22 us (3%)
    all_to_all x1, blocking collectives, on_device(): lax.all_to_all(jnp.concatenate([pieces, packed], axis=1), 'y', 0, 0, tile...  19.1 us
    all_to_all x1, blocking collectives, on_device(): lax.all_to_all(jnp.concatenate([out, extra], axis=1), PLANE, 0, 0, tiled=...  14.9 us
    all_to_all x1, starting transfers between devices, on_device(): mine = lax.all_to_all(mine, 'zh', 0, 0, tiled=True)  14.5 us
    all_to_all x1, waiting for transfers between devices, on_device(): strip = lax.all_to_all(strip, 'x', 0, 0, tiled=True)  8.09 us
    all_to_all x1, waiting for transfers between devices, on_device(): mine = lax.all_to_all(mine, 'zh', 0, 0, tiled=True)  5.98 us
    all_to_all x1, starting transfers between devices, on_device(): strip = lax.all_to_all(strip, 'x', 0, 0, tiled=True)  4.29 us
    dot_general x2, matrix products, on_device(): jnp.dot(grad[:, c * blk:(c + 1) * blk], right_roots[c], preferred_element...  4.24 us
    ppermute x1, starting transfers between devices, on_device(): other = lax.ppermute(own, 'core', [(0, 1), (1, 0)])  1.92 us
  transfers between devices with their start and end apart: 3, of which 2 were waited for; matrix products, arithmetic and copies ran while one was open for 9% of the time, Pallas kernels for 0%

profile of v2, /device:TPU:8, one launch (start us, length us, event | category | flops | bytes accessed | tf_op | source)
XLA Modules:
  0.0 81.8 jit_solution(13170458962051427130)
XLA Ops:
  0.6 0.0 copy-start
  0.6 0.8 %copy-done = bf16[4,8,1024]{2,1,0:T(8,128)(2,1)S(1)} copy-done((bf16[4,8,1024]{2,1,0:T(8,128)(2,1)S(1)}, bf16[4,8,1024]{2,1,0:T(8,128)(2,1)}, u32[]{:S(2)}) %copy-start) | copy-done | bytes 65560
  1.5 0.6 constant_dynamic-slice_fusion
  2.1 14.5 %all-to-all-start = ((bf16[4,8,512]{2,1,0:T(8,128)(2,1)}), bf16[4,8,512]{2,1,0:T(8,128)(2,1)S(1)}, u32[]{:S(2)}, u32[]{:S(2)}) async-start(bf16[4,8,512]{2,1,0:T(8,128)(2,1)} %constant_dynamic-slice_fusion), calls=%async_computation | async-start | bytes 65536 | tf_op jit(solution)/shard_map/all_to_all | solution.py:26
  16.6 0.0 copy-start.1
  16.6 0.0 copy-start.2
  16.6 2.1 %fusion.6 = bf16[32,1024]{1,0:T(8,128)(2,1)S(1)} fusion(bf16[2,1024,1024]{2,1,0:T(8,128)(2,1)} %param.9, bf16[32,2048]{1,0:T(8,128)(2,1)} %param.6), kind=kOutput, calls=%fused_computation.7 | convolution fusion | flops 67141632 | bytes 2228224 | tf_op jit(solution)/shard_map/dot_general | solution.py:36
  18.7 2.1 %fusion.9 = bf16[32,1024]{1,0:T(8,128)(2,1)S(1)} fusion(bf16[2,1024,1024]{2,1,0:T(8,128)(2,1)} %param.9, bf16[32,2048]{1,0:T(8,128)(2,1)} %param.6), kind=kOutput, calls=%fused_computation.8 | convolution fusion | flops 67141632 | bytes 2228224 | tf_op jit(solution)/shard_map/dot_general | solution.py:36
  20.9 6.0 %all-to-all-done = bf16[4,8,512]{2,1,0:T(8,128)(2,1)S(1)} async-done(((bf16[4,8,512]{2,1,0:T(8,128)(2,1)}), bf16[4,8,512]{2,1,0:T(8,128)(2,1)S(1)}, u32[]{:S(2)}, u32[]{:S(2)}) %all-to-all-start) | async-done | bytes 32800 | tf_op jit(solution)/shard_map/all_to_all | solution.py:26
  26.9 19.1 %all_to_all.20 = bf16[8,96,256]{2,1,0:T(8,128)(2,1)S(1)} all-to-all(bf16[8,96,256]{2,1,0:T(8,128)(2,1)S(1)} %pad_maximum_fusion), channel_id=1, replica_groups=mesh['zh'=4,'y'=8,'x'=4,'zl'=3,'core'=2] {'y'}, dimensions={0} | all-to-all | bytes 786432 | tf_op jit(solution)/shard_map/all_to_all | solution.py:48
  46.1 1.9 %collective-permute-start = (bf16[8,64,256]{2,1,0:T(8,128)(2,1)S(1)}, bf16[8,64,256]{2,1,0:T(8,128)(2,1)S(1)}, u32[]{:S(2)}, u32[]{:S(2)}) collective-permute-start(bf16[8,64,256]{2,1,0:T(8,128)(2,1)S(1)} %slice.56), channel_id=1, source_target_pairs={{0,1},{1,0},{2,3},{3,2},{4,5},{5,4},{6,7},{7,6},{8,9},{9,8},{10,11... | collective-permute-start | bytes 786440 | tf_op jit(solution)/shard_map/ppermute | solution.py:50
  48.0 0.8 %broadcast_in_dim.23 = bf16[4,8,32,256]{3,2,1,0:T(8,128)(2,1)} broadcast(bf16[8,32,256]{2,1,0:T(8,128)(2,1)S(1)} %slice.57), dimensions={1,2,3} | broadcast | bytes 655360 | tf_op jit(solution)/shard_map/broadcast_in_dim | solution.py:51
  48.9 4.3 %all-to-all-start.2 = ((bf16[4,8,32,256]{3,2,1,0:T(8,128)(2,1)}), bf16[4,8,32,256]{3,2,1,0:T(8,128)(2,1)S(1)}, u32[]{:S(2)}, u32[]{:S(2)}) async-start(bf16[4,8,32,256]{3,2,1,0:T(8,128)(2,1)} %broadcast_in_dim.23), calls=%async_computation.2 | async-start | bytes 1048576 | tf_op jit(solution)/shard_map/all_to_all | solution.py:52
  53.2 0.0 copy-done.1
  53.2 0.0 copy-done.2
  53.2 0.8 %fusion.15 = (f32[2048]{0:T(1024)S(1)}, f32[32,2048]{1,0:T(8,128)}) fusion(bf16[32,2048]{1,0:T(8,128)(2,1)S(1)} %copy-done.2, f32[32,2048]{1,0:T(8,128)S(1)} %copy-done.1), kind=kLoop, calls=%fused_computation.18 | loop fusion | flops 587776 | bytes 663552 | tf_op jit(solution)/shard_map/reduce_sum | solution.py:32
  54.0 0.1 reduce_sum.55
  54.2 0.0 collective-permute-done
  54.2 0.1 maximum_bitcast_fusion
  54.3 0.6 copy.37
  54.8 0.4 reshape.175
  55.2 8.1 %all-to-all-done.2 = bf16[4,8,32,256]{3,2,1,0:T(8,128)(2,1)S(1)} async-done(((bf16[4,8,32,256]{3,2,1,0:T(8,128)(2,1)}), bf16[4,8,32,256]{3,2,1,0:T(8,128)(2,1)S(1)}, u32[]{:S(2)}, u32[]{:S(2)}) %all-to-all-start.2) | async-done | bytes 524320 | tf_op jit(solution)/shard_map/all_to_all | solution.py:52
  63.4 0.9 %multiply_reduce_fusion = (f32[]{:T(128)}, bf16[256,256]{1,0:T(8,128)(2,1)S(1)}) fusion(bf16[256,1024]{1,0:T(8,128)(2,1)S(1)} %reshape.175, bf16[1024,256]{1,0:T(8,128)(2,1)S(1)} %bitcast.46), kind=kOutput, calls=%fused_computation.17 | convolution fusion | flops 134479872 | bytes 1179652 | tf_op jit(solution)/shard_map/dot_general | solution.py:59
  64.3 0.7 reduce-precision_convert_fusion.1
  65.0 0.1 copy.39
  65.1 0.1 reshape.179
  65.3 14.9 %all_to_all.21 = bf16[32,24,128]{2,1,0:T(8,128)(2,1)S(1)} all-to-all(bf16[32,24,128]{2,1,0:T(8,128)(2,1)S(1)} %pad_maximum_fusion.1), channel_id=1, replica_groups=mesh['zh'=4,'y'=8,'x'=4,'zl'=3,'core'=2] {'y','x'}, dimensions={0} | all-to-all | bytes 393216 | tf_op jit(solution)/shard_map/all_to_all | solution.py:68
  80.2 0.1 copy.42
  80.3 0.1 reshape.182
  80.4 0.1 slice_reduce_fusion
  80.5 0.1 slice_reduce_fusion.1
  80.6 0.1 broadcast_in_dim.25
  80.7 0.1 mul.43
  80.8 0.1 fusion.16
  80.9 0.1 copy.41
  81.0 0.7 reshape.180
  (19 shorter events, 0.3 us)
Async XLA Ops:
  0.6 0.8 %copy-start = (bf16[4,8,1024]{2,1,0:T(8,128)(2,1)S(1)}, bf16[4,8,1024]{2,1,0:T(8,128)(2,1)}, u32[]{:S(2)}) copy-start(bf16[4,8,1024]{2,1,0:T(8,128)(2,1)} %param.8) | copy-start | bytes 196612
  2.1 24.8 %all-to-all-start = ((bf16[4,8,512]{2,1,0:T(8,128)(2,1)}), bf16[4,8,512]{2,1,0:T(8,128)(2,1)S(1)}, u32[]{:S(2)}, u32[]{:S(2)}) async-start(bf16[4,8,512]{2,1,0:T(8,128)(2,1)} %constant_dynamic-slice_fusion), calls=%async_computation | async-start | bytes 65536 | tf_op jit(solution)/shard_map/all_to_all | solution.py:26
  16.6 36.6 %copy-start.1 = (f32[32,2048]{1,0:T(8,128)S(1)}, f32[32,2048]{1,0:T(8,128)}, u32[]{:S(2)}) copy-start(f32[32,2048]{1,0:T(8,128)} %param.7) | copy-start | bytes 786436
  16.6 36.6 %copy-start.2 = (bf16[32,2048]{1,0:T(8,128)(2,1)S(1)}, bf16[32,2048]{1,0:T(8,128)(2,1)}, u32[]{:S(2)}) copy-start(bf16[32,2048]{1,0:T(8,128)(2,1)} %param.6) | copy-start | bytes 393220
  46.1 8.1 %collective-permute-start = (bf16[8,64,256]{2,1,0:T(8,128)(2,1)S(1)}, bf16[8,64,256]{2,1,0:T(8,128)(2,1)S(1)}, u32[]{:S(2)}, u32[]{:S(2)}) collective-permute-start(bf16[8,64,256]{2,1,0:T(8,128)(2,1)S(1)} %slice.56), channel_id=1, source_target_pairs={{0,1},{1,0},{2,3},{3,2},{4,5},{5,4},{6,7},{7,6},{8,9},{9,8},{10,11... | collective-permute-start | bytes 786440 | tf_op jit(solution)/shard_map/ppermute | solution.py:50
  48.9 14.4 %all-to-all-start.2 = ((bf16[4,8,32,256]{3,2,1,0:T(8,128)(2,1)}), bf16[4,8,32,256]{3,2,1,0:T(8,128)(2,1)S(1)}, u32[]{:S(2)}, u32[]{:S(2)}) async-start(bf16[4,8,32,256]{3,2,1,0:T(8,128)(2,1)} %broadcast_in_dim.23), calls=%async_computation.2 | async-start | bytes 1048576 | tf_op jit(solution)/shard_map/all_to_all | solution.py:52

commit v3 on v1

v3 whole, which is shorter than its diff:
```python
import jax
import jax.numpy as jnp
from jax import lax
from jax.experimental import pallas as pl
from jax.experimental.pallas import tpu as pltpu
from jax.sharding import Mesh, PartitionSpec as P

ZH, YY, XX = 4, 8, 4
PEERS = YY * XX
PLANE = ("y", "x")
LANES = 128
F32, BF16 = jnp.float32, jnp.bfloat16
WHOLE = pl.BlockSpec(memory_space=pltpu.VMEM)


def split3(value):
    high = value.astype(BF16).astype(F32)
    rest = value - high
    middle = rest.astype(BF16).astype(F32)
    return high, middle, rest - middle


def by_lane(values, shape):
    lane = lax.broadcasted_iota(jnp.int32, shape, len(shape) - 1)
    out = jnp.zeros(shape, F32)
    for i, value in enumerate(values):
        out = jnp.where(lane == i, value, out)
    return out


def swap_rows(groups):
    n = 32 * groups
    row = lax.broadcasted_iota(jnp.int32, (n, n), 0)
    col = lax.broadcasted_iota(jnp.int32, (n, n), 1)
    if groups == 1:
        want = ((row >> 1) & 3) * 8 + (row >> 3) * 2 + (row & 1)
    else:
        want = ((row >> 3) & 7) * 32 + ((row >> 1) & 3) * 8 + (row >> 6) * 2 + (row & 1)
    return (col == want).astype(BF16)


def pack_kernel(proj_ref, left_ref, perm_ref, out_ref):
    rows, width = proj_ref.shape
    cols = width // YY
    blk = left_ref.shape[2]
    flat = left_ref[...].reshape(rows, blk)
    left = jnp.dot(perm_ref[...], flat, preferred_element_type=F32)
    sub = rows // XX
    for q in range(XX):
        piece = left[q * sub : (q + 1) * sub]
        tall = [piece[:, h * cols : (h + 1) * cols] for h in range(blk // cols)]
        piece = jnp.concatenate(tall, axis=0).astype(BF16)
        for j in range(YY):
            out_ref[j * XX + q, rows:, :] = piece
    for j in range(YY):
        piece = proj_ref[:, j * cols : (j + 1) * cols]
        for q in range(XX):
            out_ref[j * XX + q, :rows, :] = piece


def product_kernel(got_ref, perm_ref, adam_ref, out_ref):
    peers, both, cols = got_ref.shape
    rows = both // 2
    sub = rows // XX
    tall = got_ref[:, :rows, :].reshape(peers * rows, cols)
    total = jnp.zeros((peers * sub, cols), F32)
    for g in range(2):
        pair = got_ref[:, rows + g * 16 : rows + (g + 1) * 16, :].reshape(peers * 16, cols)
        for h in range(2):
            k = (2 * g + h) * cols
            part = jnp.dot(pair, tall[k : k + cols], preferred_element_type=F32)
            part = part.reshape(peers, 2, sub, cols)[:, h]
            total = total + part.reshape(peers * sub, cols)
    mixed = total.astype(BF16)
    again = mixed.astype(F32)
    square = jnp.sum(jnp.sum(again * again, axis=0, keepdims=True), axis=1, keepdims=True)
    sums = by_lane(split3(square), (1, LANES)) + adam_ref[...]
    out_ref[:, :, cols:] = jnp.broadcast_to(sums.astype(BF16)[None], (peers, sub, LANES))
    turned = jnp.dot(perm_ref[...], mixed, preferred_element_type=F32).astype(BF16)
    out_ref[:, :, :cols] = turned.reshape(peers, sub, cols)


def update_kernel(col_blocks, back_ref, perm_ref, out_ref):
    peers, sub, both = back_ref.shape
    cols = both - LANES
    back = back_ref[...].astype(F32)
    sums = back[:, 0, cols:]
    lane = lax.broadcasted_iota(jnp.int32, (1, LANES), 1)
    every = jnp.sum(sums, axis=0, keepdims=True)
    share = peers // col_blocks
    for c in range(col_blocks):
        own = jnp.sum(sums[c * share : (c + 1) * share], axis=0, keepdims=True)
        mixed_sq = jnp.sum(jnp.where(lane < 3, own, 0.0), axis=1, keepdims=True)
        here = (lane >= 3 * (c + 1)) & (lane < 3 * (c + 2))
        adam_sq = jnp.sum(jnp.where(here, every, 0.0), axis=1, keepdims=True)
        factor = jnp.sqrt(adam_sq) / (jnp.sqrt(mixed_sq) + 1e-06)
        for j in range(c * YY // col_blocks, (c + 1) * YY // col_blocks):
            piece = back[j * XX : (j + 1) * XX, :, :cols].reshape(XX * sub, cols)
            piece = jnp.dot(perm_ref[...], piece.astype(BF16), preferred_element_type=F32)
            out_ref[:, j * cols : (j + 1) * cols] = (piece * factor).astype(BF16)


def on_device(grad, second_moment, left_roots, right_roots):
    rows, width = grad.shape
    col_blocks, blk = right_roots.shape[:2]
    cols = width // YY
    sub = rows // XX
    mine = lax.all_to_all(left_roots, "zh", 0, 0, tiled=True)

    projected = jnp.concatenate(
        [
            jnp.dot(
                grad[:, c * blk : (c + 1) * blk],
                right_roots[c],
                preferred_element_type=F32,
            ).astype(BF16)
            for c in range(col_blocks)
        ],
        axis=1,
    )
    wide = grad.astype(F32)
    moment_next = 0.95 * second_moment + 0.05 * wide * wide
    adam = wide / (jnp.sqrt(moment_next) + 1e-08)
    adam_part = jnp.sum((adam * adam).reshape(rows, col_blocks, blk), axis=(0, 2))
    high = lax.reduce_precision(adam_part, 8, 7)
    middle = lax.reduce_precision(adam_part - high, 8, 7)
    adam_sums = jnp.stack([high, middle, adam_part - high - middle], axis=1).reshape(1, -1)
    adam_sums = jnp.pad(adam_sums, ((0, 0), (3, LANES - 3 - adam_sums.shape[1])))

    send = pl.pallas_call(
        pack_kernel,
        out_shape=jax.ShapeDtypeStruct((PEERS, 2 * rows, cols), BF16),
        in_specs=[WHOLE] * 3,
        out_specs=WHOLE,
        name="pack",
        cost_estimate=pl.CostEstimate(flops=2**21, bytes_accessed=2**21, transcendentals=0),
    )(projected, mine, swap_rows(1))
    got = lax.all_to_all(send, PLANE, 0, 0, tiled=True)
    ready = pl.pallas_call(
        product_kernel,
        out_shape=jax.ShapeDtypeStruct((PEERS, sub, cols + LANES), BF16),
        in_specs=[WHOLE] * 3,
        out_specs=WHOLE,
        name="product",
        cost_estimate=pl.CostEstimate(flops=2**28, bytes_accessed=2**21, transcendentals=0),
    )(got, swap_rows(YY), adam_sums)
    back = lax.all_to_all(ready, PLANE, 0, 0, tiled=True)
    update = pl.pallas_call(
        lambda *refs: update_kernel(col_blocks, *refs),
        out_shape=jax.ShapeDtypeStruct((rows, width), BF16),
        in_specs=[WHOLE] * 2,
        out_specs=WHOLE,
        name="update",
        cost_estimate=pl.CostEstimate(flops=2**22, bytes_accessed=2**19, transcendentals=0),
    )(back, swap_rows(1))
    return (update, moment_next)


def solution(mesh):
    tensor = mesh.shape["tensor"]
    fine = Mesh(mesh.devices.reshape(ZH, YY, XX, tensor), ("zh", "y", "x", "tensor"))
    dp = ("zh", "y", "x")
    return jax.shard_map(
        on_device,
        mesh=fine,
        in_specs=(
            P(dp, "tensor"),
            P(dp, "tensor"),
            P(None, dp, None),
            P("tensor", None, None),
        ),
        out_specs=(P(dp, "tensor"), P(dp, "tensor")),
        check_vma=False,
    )
```

time: 95.3 us -> 87.1 us (0.914)
  the two profiles are of different devices: /device:TPU:64 before, /device:TPU:8 now
where the time goes in v3:
time: 87.1 us; the launch traced here: 86.6 us
  waiting for transfers between devices  28.5 us (33%)
  starting transfers between devices  24.8 us (28%)
  blocking collectives  16.4 us (19%)
  Pallas kernels  6.47 us (7%)
  matrix products  4.19 us (5%)
  other arithmetic  3.1 us (4%)
  local copies, waits for them, and re-layouts  2.45 us (3%)
    all_to_all x1, waiting for transfers between devices, on_device(): got = lax.all_to_all(send, PLANE, 0, 0, tiled=True)  23.3 us
    all_to_all x1, blocking collectives, on_device(): back = lax.all_to_all(ready, PLANE, 0, 0, tiled=True)  16.4 us
    all_to_all x1, starting transfers between devices, on_device(): mine = lax.all_to_all(left_roots, 'zh', 0, 0, tiled=True)  14.6 us
    all_to_all x1, starting transfers between devices, on_device(): got = lax.all_to_all(send, PLANE, 0, 0, tiled=True)  10.2 us
    all_to_all x1, waiting for transfers between devices, on_device(): mine = lax.all_to_all(left_roots, 'zh', 0, 0, tiled=True)  5.24 us
    dot_general x2, matrix products, on_device(): jnp.dot(grad[:, c * blk:(c + 1) * blk], right_roots[c], preferred_element...  4.19 us
    pallas_call x1, Pallas kernels, on_device(): pl.pallas_call(product_kernel, out_shape=jax.ShapeDtypeStruct((PEERS, sub...  2.65 us
    pallas_call x1, Pallas kernels, on_device(): pl.pallas_call(pack_kernel, out_shape=jax.ShapeDtypeStruct((PEERS, 2 * ro...  2.08 us
  transfers between devices with their start and end apart: 2, of which 2 were waited for; matrix products, arithmetic and copies ran while one was open for 9% of the time, Pallas kernels for 0%

profile of v3, /device:TPU:8, one launch (start us, length us, event | category | flops | bytes accessed | tf_op | source)
XLA Modules:
  0.0 86.6 jit_solution(16064367017690150830)
XLA Ops:
  0.6 0.0 copy-start.3
  0.6 0.0 copy-start.2
  0.7 14.6 %all-to-all-start = ((bf16[4,8,1024]{2,1,0:T(8,128)(2,1)}), bf16[4,8,1024]{2,1,0:T(8,128)(2,1)S(1)}, u32[]{:S(2)}, u32[]{:S(2)}) async-start(bf16[4,8,1024]{2,1,0:T(8,128)(2,1)} %param.6), calls=%async_computation | async-start | bytes 131072 | tf_op jit(solution)/shard_map/all_to_all | solution.py:108
  15.3 2.1 %fusion.9 = bf16[32,1024]{1,0:T(8,128)(2,1)S(1)} fusion(bf16[2,1024,1024]{2,1,0:T(8,128)(2,1)} %param.7, bf16[32,2048]{1,0:T(8,128)(2,1)} %param.4), kind=kOutput, calls=%fused_computation.7 | convolution fusion | flops 67141632 | bytes 2228224 | tf_op jit(solution)/shard_map/dot_general | solution.py:112
  17.4 2.1 %fusion.6 = bf16[32,1024]{1,0:T(8,128)(2,1)S(1)} fusion(bf16[2,1024,1024]{2,1,0:T(8,128)(2,1)} %param.7, bf16[32,2048]{1,0:T(8,128)(2,1)} %param.4), kind=kOutput, calls=%fused_computation.6 | convolution fusion | flops 67141632 | bytes 2228224 | tf_op jit(solution)/shard_map/dot_general | solution.py:112
  19.5 0.7 pad_maximum_fusion.proj_ref
  20.2 0.7 fusion.18.perm_ref.refs_1_
  20.8 5.2 %all-to-all-done.left_ref = bf16[4,8,1024]{2,1,0:T(8,128)(2,1)S(1)} async-done(((bf16[4,8,1024]{2,1,0:T(8,128)(2,1)}), bf16[4,8,1024]{2,1,0:T(8,128)(2,1)S(1)}, u32[]{:S(2)}, u32[]{:S(2)}) %all-to-all-start) | async-done | bytes 65568 | tf_op jit(solution)/shard_map/all_to_all | solution.py:108
  26.1 0.0 copy-start.1
  26.1 0.6 copy-done.1
  26.7 2.1 %pack.1 = bf16[32,64,256]{2,1,0:T(8,128)(2,1)} custom-call(bf16[32,2048]{1,0:T(8,128)(2,1)} %pad_maximum_fusion.proj_ref, bf16[4,8,1024]{2,1,0:T(8,128)(2,1)} %copy-done.1, bf16[32,32]{1,0:T(8,128)(2,1)} %fusion.18.perm_ref.refs_1_), custom_call_target="tpu_custom_call" | custom-call | flops 2097152 | bytes 2097152 | tf_op jit(solution)/shard_map/pack/pallas_call | solution.py:130
  28.8 10.2 %all-to-all-start.1 = ((bf16[32,64,256]{2,1,0:T(8,128)(2,1)}), bf16[32,64,256]{2,1,0:T(8,128)(2,1)S(1)}, u32[]{:S(2)}, u32[]{:S(2)}) async-start(bf16[32,64,256]{2,1,0:T(8,128)(2,1)} %pack.1), calls=%async_computation.1 | async-start | bytes 2097152 | tf_op jit(solution)/shard_map/all_to_all | solution.py:138
  39.0 0.0 copy-done.3
  39.0 0.0 copy-done.2
  39.0 0.8 fusion.14
  39.8 0.1 reduce_sum.20
  40.0 0.1 copy.7
  40.1 0.1 reshape.33
  40.2 0.7 pad.4.adam_ref
  40.8 0.8 fusion.15.perm_ref
  41.6 23.3 %all-to-all-done.1.got_ref = bf16[32,64,256]{2,1,0:T(8,128)(2,1)S(1)} async-done(((bf16[32,64,256]{2,1,0:T(8,128)(2,1)}), bf16[32,64,256]{2,1,0:T(8,128)(2,1)S(1)}, u32[]{:S(2)}, u32[]{:S(2)}) %all-to-all-start.1) | async-done | bytes 1048608 | tf_op jit(solution)/shard_map/all_to_all | solution.py:138
  64.9 0.0 copy-start
  64.9 1.0 %copy-done = bf16[32,64,256]{2,1,0:T(8,128)(2,1)} copy-done((bf16[32,64,256]{2,1,0:T(8,128)(2,1)}, bf16[32,64,256]{2,1,0:T(8,128)(2,1)S(1)}, u32[]{:S(2)}) %copy-start) | copy-done | bytes 1048600
  65.8 2.6 %product.1 = bf16[32,8,384]{2,1,0:T(8,128)(2,1)} custom-call(bf16[32,64,256]{2,1,0:T(8,128)(2,1)} %copy-done, bf16[256,256]{1,0:T(8,128)(2,1)} %fusion.15.perm_ref, f32[1,128]{1,0:T(1,128)} %pad.4.adam_ref), custom_call_target="tpu_custom_call" | custom-call | flops 268435456 | bytes 2097152 | tf_op jit(solution)/shard_map/product/pallas_call | solution.py:139
  68.5 16.4 %all_to_all.15.refs_0_ = bf16[32,8,384]{2,1,0:T(8,128)(2,1)} all-to-all(bf16[32,8,384]{2,1,0:T(8,128)(2,1)} %product.1), channel_id=1, replica_groups=mesh['zh'=4,'y'=8,'x'=4,'tensor'=6] {'y','x'}, dimensions={0} | all-to-all | bytes 393216 | tf_op jit(solution)/shard_map/all_to_all | solution.py:147
  84.8 1.7 %update.1 = bf16[32,2048]{1,0:T(8,128)(2,1)} custom-call(bf16[32,8,384]{2,1,0:T(8,128)(2,1)} %all_to_all.15.refs_0_, bf16[32,32]{1,0:T(8,128)(2,1)} %fusion.18.perm_ref.refs_1_), custom_call_target="tpu_custom_call" | custom-call | flops 4194304 | bytes 524288 | tf_op jit(solution)/shard_map/update/pallas_call | solution.py:148
  (5 shorter events, 0.0 us)
Async XLA Ops:
  0.6 38.3 %copy-start.3 = (bf16[32,2048]{1,0:T(8,128)(2,1)S(1)}, bf16[32,2048]{1,0:T(8,128)(2,1)}, u32[]{:S(2)}) copy-start(bf16[32,2048]{1,0:T(8,128)(2,1)} %param.4) | copy-start | bytes 393220
  0.6 38.3 %copy-start.2 = (f32[32,2048]{1,0:T(8,128)S(1)}, f32[32,2048]{1,0:T(8,128)}, u32[]{:S(2)}) copy-start(f32[32,2048]{1,0:T(8,128)} %param.5) | copy-start | bytes 786436
  0.7 25.4 %all-to-all-start = ((bf16[4,8,1024]{2,1,0:T(8,128)(2,1)}), bf16[4,8,1024]{2,1,0:T(8,128)(2,1)S(1)}, u32[]{:S(2)}, u32[]{:S(2)}) async-start(bf16[4,8,1024]{2,1,0:T(8,128)(2,1)} %param.6), calls=%async_computation | async-start | bytes 131072 | tf_op jit(solution)/shard_map/all_to_all | solution.py:108
  26.1 0.6 copy-start.1
  28.8 36.1 %all-to-all-start.1 = ((bf16[32,64,256]{2,1,0:T(8,128)(2,1)}), bf16[32,64,256]{2,1,0:T(8,128)(2,1)S(1)}, u32[]{:S(2)}, u32[]{:S(2)}) async-start(bf16[32,64,256]{2,1,0:T(8,128)(2,1)} %pack.1), calls=%async_computation.1 | async-start | bytes 2097152 | tf_op jit(solution)/shard_map/all_to_all | solution.py:138
  64.9 1.0 %copy-start = (bf16[32,64,256]{2,1,0:T(8,128)(2,1)}, bf16[32,64,256]{2,1,0:T(8,128)(2,1)S(1)}, u32[]{:S(2)}) copy-start(bf16[32,64,256]{2,1,0:T(8,128)(2,1)S(1)} %all-to-all-done.1.got_ref) | copy-start | bytes 3145732

commit v4 on v3

v4 whole, which is shorter than its diff:
```python
import jax
import jax.numpy as jnp
from jax import lax
from jax.experimental import pallas as pl
from jax.experimental.pallas import tpu as pltpu
from jax.sharding import Mesh, PartitionSpec as P

ZH, YY, XX = 4, 8, 4
PEERS = YY * XX
PLANE = ("y", "x")
LANES = 128
F32, BF16 = jnp.float32, jnp.bfloat16
SMALL = pltpu.CompilerParams(vmem_limit_bytes=16 * 2**20)
WHOLE = pl.BlockSpec(memory_space=pltpu.VMEM)


def split3(value):
    high = value.astype(BF16).astype(F32)
    rest = value - high
    middle = rest.astype(BF16).astype(F32)
    return high, middle, rest - middle


def by_lane(values, shape):
    lane = lax.broadcasted_iota(jnp.int32, shape, len(shape) - 1)
    out = jnp.zeros(shape, F32)
    for i, value in enumerate(values):
        out = jnp.where(lane == i, value, out)
    return out


def right_kernel(grad_ref, right_ref, out_ref):
    both = jnp.dot(grad_ref[...], right_ref[0], preferred_element_type=F32).astype(BF16)
    cols = out_ref.shape[2]
    for i in range(both.shape[1] // cols):
        out_ref[i] = both[:, i * cols : (i + 1) * cols]


def pack_kernel(piece_ref, left_ref, out_ref):
    rows, cols = piece_ref.shape[1:]
    planes, sub, blk = left_ref.shape
    n = planes * sub
    left = left_ref[...].reshape(n, blk)
    for j in range(YY):
        out_ref[j, :rows] = piece_ref[j]
        for h in range(blk // cols):
            out_ref[j, rows + h * n : rows + (h + 1) * n] = left[:, h * cols : (h + 1) * cols]


def product_kernel(strip_ref, got_ref, adam_ref, out_ref):
    rows, cols = strip_ref.shape[2:]
    sub = rows // XX
    n = ZH * sub
    steps = (got_ref.shape[1] - rows) // n
    total = jnp.zeros((YY * n, cols), F32)
    for h in range(steps):
        left = got_ref[:, rows + h * n : rows + (h + 1) * n, :].reshape(YY * n, cols)
        per = cols // (XX * rows)
        tall = [strip_ref[i, h * per + j] for j in range(per) for i in range(XX)]
        tall = jnp.concatenate(tall, axis=0)
        total = total + jnp.dot(left, tall, preferred_element_type=F32)
    mixed = total.astype(BF16).astype(F32)
    square = jnp.sum(jnp.sum(mixed * mixed, axis=0, keepdims=True), axis=1, keepdims=True)
    sums = by_lane(split3(square), (1, LANES)) + adam_ref[...]
    sums = jnp.broadcast_to(sums, (sub, LANES))
    for y in range(YY):
        for z in range(ZH):
            m = (y * ZH + z) * sub
            piece = jnp.concatenate([mixed[m : m + sub], sums], axis=1)
            out_ref[z * YY + y] = piece.astype(BF16)


def update_kernel(col_blocks, back_ref, out_ref):
    peers, sub, both = back_ref.shape
    cols = both - LANES
    back = back_ref[...].astype(F32)
    sums = back[:, 0, cols:]
    lane = lax.broadcasted_iota(jnp.int32, (1, LANES), 1)
    every = jnp.sum(sums, axis=0, keepdims=True)
    share = peers // col_blocks
    for c in range(col_blocks):
        own = jnp.sum(sums[c * share : (c + 1) * share], axis=0, keepdims=True)
        mixed_sq = jnp.sum(jnp.where(lane < 3, own, 0.0), axis=1, keepdims=True)
        here = (lane >= 3 * (c + 1)) & (lane < 3 * (c + 2))
        adam_sq = jnp.sum(jnp.where(here, every, 0.0), axis=1, keepdims=True)
        factor = jnp.sqrt(adam_sq) / (jnp.sqrt(mixed_sq) + 1e-06)
        for j in range(c * YY // col_blocks, (c + 1) * YY // col_blocks):
            piece = back[j * XX : (j + 1) * XX, :, :cols].reshape(XX * sub, cols)
            out_ref[:, j * cols : (j + 1) * cols] = (piece * factor).astype(BF16)


def on_device(grad, second_moment, left_roots, right_roots):
    rows, width = grad.shape
    col_blocks, blk = right_roots.shape[:2]
    cols = width // YY
    sub = rows // XX
    mine = lax.all_to_all(left_roots, "zh", 0, 0, tiled=True)
    wide_cols = width // 4
    per_block = blk // wide_cols
    pieces = pl.pallas_call(
        right_kernel,
        grid=(4,),
        out_shape=jax.ShapeDtypeStruct((YY, rows, cols), BF16),
        in_specs=[
            pl.BlockSpec((rows, blk), lambda s: (0, s // per_block)),
            pl.BlockSpec((1, blk, wide_cols), lambda s: (s // per_block, 0, s % per_block)),
        ],
        out_specs=pl.BlockSpec((YY // 4, rows, cols), lambda s: (s, 0, 0)),
        name="right",
        compiler_params=pltpu.CompilerParams(vmem_limit_bytes=57 * 2**20),
        cost_estimate=pl.CostEstimate(flops=2**27, bytes_accessed=2**22, transcendentals=0),
    )(grad, right_roots)
    wide = grad.astype(F32)
    moment_next = 0.95 * second_moment + 0.05 * wide * wide
    adam = wide / (jnp.sqrt(moment_next) + 1e-08)
    adam_part = jnp.sum((adam * adam).reshape(rows, col_blocks, blk), axis=(0, 2))
    high = lax.reduce_precision(adam_part, 8, 7)
    middle = lax.reduce_precision(adam_part - high, 8, 7)
    adam_sums = jnp.stack([high, middle, adam_part - high - middle], axis=1).reshape(1, -1)
    adam_sums = jnp.pad(adam_sums, ((0, 0), (3, LANES - 3 - adam_sums.shape[1])))

    send = pl.pallas_call(
        pack_kernel,
        out_shape=jax.ShapeDtypeStruct((YY, rows + ZH * sub * blk // cols, cols), BF16),
        in_specs=[WHOLE] * 2,
        out_specs=WHOLE,
        name="pack",
        compiler_params=SMALL,
        cost_estimate=pl.CostEstimate(flops=2**10, bytes_accessed=2**20, transcendentals=0),
    )(pieces, mine)
    got = lax.all_to_all(send, "y", 0, 0, tiled=True)
    strip = jnp.broadcast_to(got[None, :, :rows], (XX, YY, rows, cols))
    strip = lax.all_to_all(strip, "x", 0, 0, tiled=True)
    ready = pl.pallas_call(
        product_kernel,
        out_shape=jax.ShapeDtypeStruct((PEERS, sub, cols + LANES), BF16),
        in_specs=[WHOLE] * 3,
        out_specs=WHOLE,
        name="product",
        compiler_params=SMALL,
        cost_estimate=pl.CostEstimate(flops=2**28, bytes_accessed=2**21, transcendentals=0),
    )(strip, got, adam_sums)
    back = lax.all_to_all(ready, PLANE, 0, 0, tiled=True)
    update = pl.pallas_call(
        lambda *refs: update_kernel(col_blocks, *refs),
        out_shape=jax.ShapeDtypeStruct((rows, width), BF16),
        in_specs=[WHOLE],
        out_specs=WHOLE,
        name="update",
        compiler_params=SMALL,
        cost_estimate=pl.CostEstimate(flops=2**22, bytes_accessed=2**19, transcendentals=0),
    )(back)
    return (update, moment_next)


def solution(mesh):
    tensor = mesh.shape["tensor"]
    fine = Mesh(mesh.devices.reshape(ZH, YY, XX, tensor), ("zh", "y", "x", "tensor"))
    dp = ("zh", "y", "x")
    return jax.shard_map(
        on_device,
        mesh=fine,
        in_specs=(
            P(dp, "tensor"),
            P(dp, "tensor"),
            P(None, dp, None),
            P("tensor", None, None),
        ),
        out_specs=(P(dp, "tensor"), P(dp, "tensor")),
        check_vma=False,
    )
```

time: 87.1 us -> 80.7 us (0.927)
  blocking collectives: 16.4 us -> 38.9 us
  waiting for transfers between devices: 28.5 us -> 13.1 us
  starting transfers between devices: 24.8 us -> 18.8 us
  matrix products: 4.19 us -> 0 us
  other arithmetic: 3.1 us -> 0.99 us
    all_to_all x0 -> x1, blocking collectives: none -> 24.6 us  [on_device(): got = lax.all_to_all(send, 'y', 0, 0, tiled=True)]
    all_to_all x1, waiting for transfers between devices: 23.3 us -> 6.82 us  [on_device(): strip = lax.all_to_all(strip, 'x', 0, 0, tiled=True)]
    all_to_all x1, starting transfers between devices: 10.2 us -> 4.29 us  [on_device(): strip = lax.all_to_all(strip, 'x', 0, 0, tiled=True)]
    dot_general x2 -> x0, matrix products: 4.19 us -> none  [on_device(): jnp.dot(grad[:, c * blk:(c + 1) * blk], right_roots[c], preferred_element...]
    pallas_call x1 -> x2, Pallas kernels: 2.08 us -> 4.55 us  [the longest x1 4.51 us: on_device(): pl.pallas_call(right_kernel, grid=(4,), out_shape=jax.ShapeDtypeStruct((Y...]
    pallas_call x1, Pallas kernels: 2.65 us -> 0.41 us  [on_device(): pl.pallas_call(product_kernel, out_shape=jax.ShapeDtypeStruct((PEERS, sub...]
    all_to_all x1, blocking collectives: 16.4 us -> 14.4 us  [on_device(): back = lax.all_to_all(ready, PLANE, 0, 0, tiled=True)]
    convert_element_type x2 -> x0, other arithmetic: 1.42 us -> none  [swap_rows(): return (col == want).astype(BF16)]
  transfers between devices with their start and end apart: 2 -> 2, of which waited for: 2 -> 2; matrix products, arithmetic and copies ran while one was open for 9% -> 2% of each run, Pallas kernels for 0% -> 6%
where the time goes in v4:
time: 80.7 us; the launch traced here: 80.2 us
  blocking collectives  38.9 us (48%)
  starting transfers between devices  18.8 us (23%)
  waiting for transfers between devices  13.1 us (16%)
  Pallas kernels  5.74 us (7%)
  local copies, waits for them, and re-layouts  2.04 us (3%)
  other arithmetic  0.99 us (1%)
    all_to_all x1, blocking collectives, on_device(): got = lax.all_to_all(send, 'y', 0, 0, tiled=True)  24.6 us
    all_to_all x1, starting transfers between devices, on_device(): mine = lax.all_to_all(left_roots, 'zh', 0, 0, tiled=True)  14.5 us
    all_to_all x1, blocking collectives, on_device(): back = lax.all_to_all(ready, PLANE, 0, 0, tiled=True)  14.4 us
    all_to_all x1, waiting for transfers between devices, on_device(): strip = lax.all_to_all(strip, 'x', 0, 0, tiled=True)  6.82 us
    all_to_all x1, waiting for transfers between devices, on_device(): mine = lax.all_to_all(left_roots, 'zh', 0, 0, tiled=True)  6.27 us
    pallas_call x1, Pallas kernels, on_device(): pl.pallas_call(right_kernel, grid=(4,), out_shape=jax.ShapeDtypeStruct((Y...  4.51 us
    all_to_all x1, starting transfers between devices, on_device(): strip = lax.all_to_all(strip, 'x', 0, 0, tiled=True)  4.29 us
  transfers between devices with their start and end apart: 2, of which 2 were waited for; matrix products, arithmetic and copies ran while one was open for 2% of the time, Pallas kernels for 6%

profile of v4, /device:TPU:8, one launch (start us, length us, event | category | flops | bytes accessed | tf_op | source)
XLA Modules:
  0.0 80.2 jit_solution(16242840520911574234)
XLA Ops:
  0.6 14.5 %all-to-all-start = ((bf16[4,8,1024]{2,1,0:T(8,128)(2,1)}), bf16[4,8,1024]{2,1,0:T(8,128)(2,1)S(1)}, u32[]{:S(2)}, u32[]{:S(2)}) async-start(bf16[4,8,1024]{2,1,0:T(8,128)(2,1)} %param.6), calls=%async_computation | async-start | bytes 131072 | tf_op jit(solution)/shard_map/all_to_all | solution.py:97
  15.1 0.0 copy-start.1
  15.1 0.0 copy-start.2
  15.1 4.5 %right.1.piece_ref = bf16[8,32,256]{2,1,0:T(8,128)(2,1)} custom-call(bf16[32,2048]{1,0:T(8,128)(2,1)} %grad_ref.1, bf16[2,1024,1024]{2,1,0:T(8,128)(2,1)} %right_ref.1), custom_call_target="tpu_custom_call" | custom-call | flops 134217728 | bytes 4194304 | tf_op jit(solution)/shard_map/right/pallas_call | solution.py:100
  19.7 6.3 %all-to-all-done.left_ref = bf16[4,8,1024]{2,1,0:T(8,128)(2,1)S(1)} async-done(((bf16[4,8,1024]{2,1,0:T(8,128)(2,1)}), bf16[4,8,1024]{2,1,0:T(8,128)(2,1)S(1)}, u32[]{:S(2)}, u32[]{:S(2)}) %all-to-all-start) | async-done | bytes 65568 | tf_op jit(solution)/shard_map/all_to_all | solution.py:97
  25.9 0.0 copy-start
  25.9 0.9 %copy-done = bf16[8,32,256]{2,1,0:T(8,128)(2,1)S(1)} copy-done((bf16[8,32,256]{2,1,0:T(8,128)(2,1)S(1)}, bf16[8,32,256]{2,1,0:T(8,128)(2,1)}, u32[]{:S(2)}) %copy-start) | copy-done | bytes 131096
  26.9 24.6 %all_to_all.20.got_ref = bf16[8,160,256]{2,1,0:T(8,128)(2,1)S(1)} all-to-all(bf16[8,160,256]{2,1,0:T(8,128)(2,1)S(1)} %pack.1), channel_id=1, replica_groups=mesh['zh'=4,'y'=8,'x'=4,'tensor'=6] {'y'}, dimensions={0} | all-to-all | bytes 1310720 | tf_op jit(solution)/shard_map/all_to_all | solution.py:131
  51.4 0.9 %broadcast_in_dim.2 = bf16[4,8,32,256]{3,2,1,0:T(8,128)(2,1)} broadcast(bf16[8,32,256]{2,1,0:T(8,128)(2,1)S(1)} %slice.4), dimensions={1,2,3} | broadcast | bytes 655360 | tf_op jit(solution)/shard_map/broadcast_in_dim | solution.py:132
  52.3 4.3 %all-to-all-start.2 = ((bf16[4,8,32,256]{3,2,1,0:T(8,128)(2,1)}), bf16[4,8,32,256]{3,2,1,0:T(8,128)(2,1)S(1)}, u32[]{:S(2)}, u32[]{:S(2)}) async-start(bf16[4,8,32,256]{3,2,1,0:T(8,128)(2,1)} %broadcast_in_dim.2), calls=%async_computation.2 | async-start | bytes 1048576 | tf_op jit(solution)/shard_map/all_to_all | solution.py:133
  56.6 0.0 copy-done.1
  56.6 0.0 copy-done.2
  56.6 0.8 %fusion.2 = (f32[2048]{0:T(1024)S(1)}, f32[32,2048]{1,0:T(8,128)}) fusion(bf16[32,2048]{1,0:T(8,128)(2,1)S(1)} %copy-done.1, f32[32,2048]{1,0:T(8,128)S(1)} %copy-done.2), kind=kLoop, calls=%fused_computation.4 | loop fusion | flops 587776 | bytes 663552 | tf_op jit(solution)/shard_map/reduce_sum | solution.py:116
  57.5 0.1 reduce_sum.20
  57.6 0.1 copy.7
  57.7 0.1 reshape.34
  57.8 0.1 pad.4.adam_ref
  57.9 6.8 %all-to-all-done.2.strip_ref = bf16[4,8,32,256]{3,2,1,0:T(8,128)(2,1)S(1)} async-done(((bf16[4,8,32,256]{3,2,1,0:T(8,128)(2,1)}), bf16[4,8,32,256]{3,2,1,0:T(8,128)(2,1)S(1)}, u32[]{:S(2)}, u32[]{:S(2)}) %all-to-all-start.2) | async-done | bytes 524320 | tf_op jit(solution)/shard_map/all_to_all | solution.py:133
  64.7 0.4 product.1
  65.1 14.4 %all_to_all.21.refs_0_ = bf16[32,8,384]{2,1,0:T(8,128)(2,1)S(1)} all-to-all(bf16[32,8,384]{2,1,0:T(8,128)(2,1)S(1)} %product.1), channel_id=1, replica_groups=mesh['zh'=4,'y'=8,'x'=4,'tensor'=6] {'y','x'}, dimensions={0} | all-to-all | bytes 393216 | tf_op jit(solution)/shard_map/all_to_all | solution.py:143
  79.5 0.8 update.1
  (5 shorter events, 0.1 us)
Async XLA Ops:
  0.6 25.3 %all-to-all-start = ((bf16[4,8,1024]{2,1,0:T(8,128)(2,1)}), bf16[4,8,1024]{2,1,0:T(8,128)(2,1)S(1)}, u32[]{:S(2)}, u32[]{:S(2)}) async-start(bf16[4,8,1024]{2,1,0:T(8,128)(2,1)} %param.6), calls=%async_computation | async-start | bytes 131072 | tf_op jit(solution)/shard_map/all_to_all | solution.py:97
  15.1 41.5 %copy-start.1 = (bf16[32,2048]{1,0:T(8,128)(2,1)S(1)}, bf16[32,2048]{1,0:T(8,128)(2,1)}, u32[]{:S(2)}) copy-start(bf16[32,2048]{1,0:T(8,128)(2,1)} %grad_ref.1) | copy-start | bytes 393220
  15.1 41.5 %copy-start.2 = (f32[32,2048]{1,0:T(8,128)S(1)}, f32[32,2048]{1,0:T(8,128)}, u32[]{:S(2)}) copy-start(f32[32,2048]{1,0:T(8,128)} %param.5) | copy-start | bytes 786436
  25.9 0.9 %copy-start = (bf16[8,32,256]{2,1,0:T(8,128)(2,1)S(1)}, bf16[8,32,256]{2,1,0:T(8,128)(2,1)}, u32[]{:S(2)}) copy-start(bf16[8,32,256]{2,1,0:T(8,128)(2,1)} %right.1.piece_ref) | copy-start | bytes 393220
  52.3 12.4 %all-to-all-start.2 = ((bf16[4,8,32,256]{3,2,1,0:T(8,128)(2,1)}), bf16[4,8,32,256]{3,2,1,0:T(8,128)(2,1)S(1)}, u32[]{:S(2)}, u32[]{:S(2)}) async-start(bf16[4,8,32,256]{3,2,1,0:T(8,128)(2,1)} %broadcast_in_dim.2), calls=%async_computation.2 | async-start | bytes 1048576 | tf_op jit(solution)/shard_map/all_to_all | solution.py:133

commit v5 on v4

--- a/solution.py
+++ b/solution.py
@@ -11,6 +11,7 @@
 LANES = 128
 F32, BF16 = jnp.float32, jnp.bfloat16
 SMALL = pltpu.CompilerParams(vmem_limit_bytes=16 * 2**20)
+SCALARS = pl.BlockSpec(memory_space=pltpu.SMEM)
 WHOLE = pl.BlockSpec(memory_space=pltpu.VMEM)
 
 
@@ -36,29 +37,31 @@
         out_ref[i] = both[:, i * cols : (i + 1) * cols]
 
 
-def pack_kernel(piece_ref, left_ref, out_ref):
+def pack_kernel(core_ref, piece_ref, left_ref, out_ref):
     rows, cols = piece_ref.shape[1:]
     planes, sub, blk = left_ref.shape
     n = planes * sub
+    half = blk // 2
     left = left_ref[...].reshape(n, blk)
+    left = jnp.where(core_ref[0] == 0, left[:, :half], left[:, half:])
     for j in range(YY):
         out_ref[j, :rows] = piece_ref[j]
-        for h in range(blk // cols):
+        for h in range(half // cols):
             out_ref[j, rows + h * n : rows + (h + 1) * n] = left[:, h * cols : (h + 1) * cols]
 
 
-def product_kernel(strip_ref, got_ref, adam_ref, out_ref):
+def product_kernel(strip_ref, left_ref, adam_ref, out_ref):
     rows, cols = strip_ref.shape[2:]
     sub = rows // XX
     n = ZH * sub
-    steps = (got_ref.shape[1] - rows) // n
+    steps = left_ref.shape[2] // n
+    per = cols // (XX * rows)
     total = jnp.zeros((YY * n, cols), F32)
-    for h in range(steps):
-        left = got_ref[:, rows + h * n : rows + (h + 1) * n, :].reshape(YY * n, cols)
-        per = cols // (XX * rows)
+    for h in range(2 * steps):
+        left = left_ref[h // steps, :, h % steps * n : (h % steps + 1) * n, :]
         tall = [strip_ref[i, h * per + j] for j in range(per) for i in range(XX)]
         tall = jnp.concatenate(tall, axis=0)
-        total = total + jnp.dot(left, tall, preferred_element_type=F32)
+        total = total + jnp.dot(left.reshape(YY * n, cols), tall, preferred_element_type=F32)
     mixed = total.astype(BF16).astype(F32)
     square = jnp.sum(jnp.sum(mixed * mixed, axis=0, keepdims=True), axis=1, keepdims=True)
     sums = by_lane(split3(square), (1, LANES)) + adam_ref[...]
@@ -107,7 +110,7 @@
         ],
         out_specs=pl.BlockSpec((YY // 4, rows, cols), lambda s: (s, 0, 0)),
         name="right",
-        compiler_params=pltpu.CompilerParams(vmem_limit_bytes=57 * 2**20),
+        compiler_params=SMALL,
         cost_estimate=pl.CostEstimate(flops=2**27, bytes_accessed=2**22, transcendentals=0),
     )(grad, right_roots)
     wide = grad.astype(F32)
@@ -121,14 +124,15 @@
 
     send = pl.pallas_call(
         pack_kernel,
-        out_shape=jax.ShapeDtypeStruct((YY, rows + ZH * sub * blk // cols, cols), BF16),
-        in_specs=[WHOLE] * 2,
+        out_shape=jax.ShapeDtypeStruct((YY, rows + ZH * sub * blk // (2 * cols), cols), BF16),
+        in_specs=[SCALARS] + [WHOLE] * 2,
         out_specs=WHOLE,
         name="pack",
         compiler_params=SMALL,
         cost_estimate=pl.CostEstimate(flops=2**10, bytes_accessed=2**20, transcendentals=0),
-    )(pieces, mine)
+    )(lax.axis_index("core")[None], pieces, mine)
     got = lax.all_to_all(send, "y", 0, 0, tiled=True)
+    left = lax.all_gather(got[:, rows:], "core", axis=0)
     strip = jnp.broadcast_to(got[None, :, :rows], (XX, YY, rows, cols))
     strip = lax.all_to_all(strip, "x", 0, 0, tiled=True)
     ready = pl.pallas_call(
@@ -139,7 +143,7 @@
         name="product",
         compiler_params=SMALL,
         cost_estimate=pl.CostEstimate(flops=2**28, bytes_accessed=2**21, transcendentals=0),
-    )(strip, got, adam_sums)
+    )(strip, left, adam_sums)
     back = lax.all_to_all(ready, PLANE, 0, 0, tiled=True)
     update = pl.pallas_call(
         lambda *refs: update_kernel(col_blocks, *refs),
@@ -155,17 +159,18 @@
 
 def solution(mesh):
     tensor = mesh.shape["tensor"]
-    fine = Mesh(mesh.devices.reshape(ZH, YY, XX, tensor), ("zh", "y", "x", "tensor"))
-    dp = ("zh", "y", "x")
+    names = ("zh", "y", "x", "zl", "core")
+    fine = Mesh(mesh.devices.reshape(ZH, YY, XX, tensor // 2, 2), names)
+    dp, columns = ("zh", "y", "x"), ("zl", "core")
     return jax.shard_map(
         on_device,
         mesh=fine,
         in_specs=(
-            P(dp, "tensor"),
-            P(dp, "tensor"),
+            P(dp, columns),
+            P(dp, columns),
             P(None, dp, None),
-            P("tensor", None, None),
+            P(columns, None, None),
         ),
-        out_specs=(P(dp, "tensor"), P(dp, "tensor")),
+        out_specs=(P(dp, columns), P(dp, columns)),
         check_vma=False,
     )

time: 80.7 us -> 75.2 us (0.932)
  blocking collectives: 38.9 us -> 16.6 us
  waiting for transfers between devices: 13.1 us -> 22.4 us
  starting transfers between devices: 18.8 us -> 26.5 us
  Pallas kernels: 5.74 us -> 3.43 us
  local copies, waits for them, and re-layouts: 2.04 us -> 4.25 us
    all_to_all x1 -> x0, blocking collectives: 24.6 us -> none  [on_device(): got = lax.all_to_all(send, 'y', 0, 0, tiled=True)]
    all_to_all x0 -> x1, waiting for transfers between devices: none -> 10.6 us  [on_device(): got = lax.all_to_all(send, 'y', 0, 0, tiled=True)]
    all_to_all x0 -> x1, starting transfers between devices: none -> 7.55 us  [on_device(): got = lax.all_to_all(send, 'y', 0, 0, tiled=True)]
    pallas_call x1, Pallas kernels: 4.51 us -> 1.45 us  [on_device(): pl.pallas_call(right_kernel, grid=(4,), out_shape=jax.ShapeDtypeStruct((Y...]
    unnamed x6 -> x8, local copies, waits for them, and re-layouts: 0.91 us -> 3.1 us
    all_gather x0 -> x1, blocking collectives: none -> 2.18 us  [on_device(): left = lax.all_gather(got[:, rows:], 'core', axis=0)]
    all_to_all x1, waiting for transfers between devices: 6.82 us -> 5.6 us  [on_device(): strip = lax.all_to_all(strip, 'x', 0, 0, tiled=True)]
  transfers between devices with their start and end apart: 2 -> 3, of which waited for: 2 -> 3; matrix products, arithmetic and copies ran while one was open for 2% -> 2% of each run, Pallas kernels for 6% -> 2%
where the time goes in v5:
time: 75.2 us; the launch traced here: 74.8 us
  starting transfers between devices  26.5 us (35%)
  waiting for transfers between devices  22.4 us (30%)
  blocking collectives  16.6 us (22%)
  local copies, waits for them, and re-layouts  4.25 us (6%)
  Pallas kernels  3.43 us (5%)
  other arithmetic  0.99 us (1%)
    all_to_all x1, starting transfers between devices, on_device(): mine = lax.all_to_all(left_roots, 'zh', 0, 0, tiled=True)  14.6 us
    all_to_all x1, blocking collectives, on_device(): back = lax.all_to_all(ready, PLANE, 0, 0, tiled=True)  14.4 us
    all_to_all x1, waiting for transfers between devices, on_device(): got = lax.all_to_all(send, 'y', 0, 0, tiled=True)  10.6 us
    all_to_all x1, starting transfers between devices, on_device(): got = lax.all_to_all(send, 'y', 0, 0, tiled=True)  7.55 us
    all_to_all x1, waiting for transfers between devices, on_device(): mine = lax.all_to_all(left_roots, 'zh', 0, 0, tiled=True)  6.24 us
    all_to_all x1, waiting for transfers between devices, on_device(): strip = lax.all_to_all(strip, 'x', 0, 0, tiled=True)  5.6 us
    all_to_all x1, starting transfers between devices, on_device(): strip = lax.all_to_all(strip, 'x', 0, 0, tiled=True)  4.29 us
    unnamed x8, local copies, waits for them, and re-layouts  3.1 us
  transfers between devices with their start and end apart: 3, of which 3 were waited for; matrix products, arithmetic and copies ran while one was open for 2% of the time, Pallas kernels for 2%

profile of v5, /device:TPU:8, one launch (start us, length us, event | category | flops | bytes accessed | tf_op | source)
XLA Modules:
  0.0 74.8 jit_solution(3753166735157560560)
XLA Ops:
  0.6 0.0 copy-start.2
  0.6 14.6 %all-to-all-start = ((bf16[4,8,1024]{2,1,0:T(8,128)(2,1)}), bf16[4,8,1024]{2,1,0:T(8,128)(2,1)S(1)}, u32[]{:S(2)}, u32[]{:S(2)}) async-start(bf16[4,8,1024]{2,1,0:T(8,128)(2,1)} %param.6), calls=%async_computation | async-start | bytes 131072 | tf_op jit(solution)/shard_map/all_to_all | solution.py:100
  15.3 0.0 copy-start
  15.3 2.2 %copy-done = bf16[2,1024,1024]{2,1,0:T(8,128)(2,1)S(1)} copy-done((bf16[2,1024,1024]{2,1,0:T(8,128)(2,1)S(1)}, bf16[2,1024,1024]{2,1,0:T(8,128)(2,1)}, u32[]{:S(2)}) %copy-start) | copy-done | bytes 4194328
  17.5 0.0 copy-start.1
  17.5 0.9 %copy-done.1 = bf16[32,2048]{1,0:T(8,128)(2,1)S(1)} copy-done((bf16[32,2048]{1,0:T(8,128)(2,1)S(1)}, bf16[32,2048]{1,0:T(8,128)(2,1)}, u32[]{:S(2)}) %copy-start.1) | copy-done | bytes 131096
  18.4 0.0 copy-start.3
  18.4 1.4 %right.1.piece_ref = bf16[8,32,256]{2,1,0:T(8,128)(2,1)S(1)} custom-call(bf16[32,2048]{1,0:T(8,128)(2,1)S(1)} %copy-done.1, bf16[2,1024,1024]{2,1,0:T(8,128)(2,1)S(1)} %copy-done), custom_call_target="tpu_custom_call" | custom-call | flops 134217728 | bytes 4194304 | tf_op jit(solution)/shard_map/right/pallas_call | solution.py:103
  19.8 6.2 %all-to-all-done.left_ref = bf16[4,8,1024]{2,1,0:T(8,128)(2,1)S(1)} async-done(((bf16[4,8,1024]{2,1,0:T(8,128)(2,1)}), bf16[4,8,1024]{2,1,0:T(8,128)(2,1)S(1)}, u32[]{:S(2)}, u32[]{:S(2)}) %all-to-all-start) | async-done | bytes 65568 | tf_op jit(solution)/shard_map/all_to_all | solution.py:100
  26.1 0.8 %pack.1 = bf16[8,96,256]{2,1,0:T(8,128)(2,1)} custom-call(s32[1]{0:T(128)} %bitcast.core_ref, bf16[8,32,256]{2,1,0:T(8,128)(2,1)S(1)} %right.1.piece_ref, bf16[4,8,1024]{2,1,0:T(8,128)(2,1)S(1)} %all-to-all-done.left_ref), custom_call_target="tpu_custom_call" | custom-call | flops 1024 | bytes 1048576 | tf_op jit(solution)/shard_map/pack/pallas_call | solution.py:125
  26.9 7.5 %all-to-all-start.1 = ((bf16[8,96,256]{2,1,0:T(8,128)(2,1)}), bf16[8,96,256]{2,1,0:T(8,128)(2,1)S(1)}, u32[]{:S(2)}, u32[]{:S(2)}) async-start(bf16[8,96,256]{2,1,0:T(8,128)(2,1)} %pack.1), calls=%async_computation.1 | async-start | bytes 786432 | tf_op jit(solution)/shard_map/all_to_all | solution.py:134
  34.4 0.0 copy-done.2
  34.4 0.0 copy-done.3
  34.4 0.8 %fusion.2 = (f32[2048]{0:T(1024)S(1)}, f32[32,2048]{1,0:T(8,128)}) fusion(bf16[32,2048]{1,0:T(8,128)(2,1)S(1)} %copy-done.2, f32[32,2048]{1,0:T(8,128)S(1)} %copy-done.3), kind=kLoop, calls=%fused_computation.4 | loop fusion | flops 587776 | bytes 663552 | tf_op jit(solution)/shard_map/reduce_sum | solution.py:119
  35.3 0.1 reduce_sum.20
  35.4 10.6 %all-to-all-done.1 = bf16[8,96,256]{2,1,0:T(8,128)(2,1)S(1)} async-done(((bf16[8,96,256]{2,1,0:T(8,128)(2,1)}), bf16[8,96,256]{2,1,0:T(8,128)(2,1)S(1)}, u32[]{:S(2)}, u32[]{:S(2)}) %all-to-all-start.1) | async-done | bytes 393248 | tf_op jit(solution)/shard_map/all_to_all | solution.py:134
  46.0 0.9 %broadcast_in_dim.10 = bf16[4,8,32,256]{3,2,1,0:T(8,128)(2,1)} broadcast(bf16[8,32,256]{2,1,0:T(8,128)(2,1)S(1)} %slice.8), dimensions={1,2,3} | broadcast | bytes 655360 | tf_op jit(solution)/shard_map/broadcast_in_dim | solution.py:136
  46.8 4.3 %all-to-all-start.2 = ((bf16[4,8,32,256]{3,2,1,0:T(8,128)(2,1)}), bf16[4,8,32,256]{3,2,1,0:T(8,128)(2,1)S(1)}, u32[]{:S(2)}, u32[]{:S(2)}) async-start(bf16[4,8,32,256]{3,2,1,0:T(8,128)(2,1)} %broadcast_in_dim.10), calls=%async_computation.2 | async-start | bytes 1048576 | tf_op jit(solution)/shard_map/all_to_all | solution.py:137
  51.1 0.1 copy.8
  51.2 0.1 reshape.34
  51.3 0.1 pad.4.adam_ref
  51.4 2.2 %all-gather = bf16[16,64,256]{2,1,0:T(8,128)(2,1)S(1)} all-gather(bf16[8,64,256]{2,1,0:T(8,128)(2,1)S(1)} %slice.9), channel_id=2, replica_groups=mesh['zh'=4,'y'=8,'x'=4,'zl'=3,'core'=2] {'core'}, dimensions={0}, use_global_device_ids=true | all-gather | bytes 786432 | tf_op jit(solution)/shard_map/all_gather | solution.py:135
  53.6 5.6 %all-to-all-done.2.strip_ref = bf16[4,8,32,256]{3,2,1,0:T(8,128)(2,1)S(1)} async-done(((bf16[4,8,32,256]{3,2,1,0:T(8,128)(2,1)}), bf16[4,8,32,256]{3,2,1,0:T(8,128)(2,1)S(1)}, u32[]{:S(2)}, u32[]{:S(2)}) %all-to-all-start.2) | async-done | bytes 524320 | tf_op jit(solution)/shard_map/all_to_all | solution.py:137
  59.2 0.4 product.1
  59.6 14.4 %all_to_all.20.refs_0_ = bf16[32,8,384]{2,1,0:T(8,128)(2,1)S(1)} all-to-all(bf16[32,8,384]{2,1,0:T(8,128)(2,1)S(1)} %product.1), channel_id=1, replica_groups=mesh['zh'=4,'y'=8,'x'=4,'zl'=3,'core'=2] {'y','x'}, dimensions={0} | all-to-all | bytes 393216 | tf_op jit(solution)/shard_map/all_to_all | solution.py:147
  74.0 0.8 %update.1 = bf16[32,2048]{1,0:T(8,128)(2,1)} custom-call(bf16[32,8,384]{2,1,0:T(8,128)(2,1)S(1)} %all_to_all.20.refs_0_), custom_call_target="tpu_custom_call" | custom-call | flops 4194304 | bytes 524288 | tf_op jit(solution)/shard_map/update/pallas_call | solution.py:148
  (5 shorter events, 0.1 us)
Async XLA Ops:
  0.6 33.8 %copy-start.2 = (bf16[32,2048]{1,0:T(8,128)(2,1)S(1)}, bf16[32,2048]{1,0:T(8,128)(2,1)}, u32[]{:S(2)}) copy-start(bf16[32,2048]{1,0:T(8,128)(2,1)} %grad_ref.1) | copy-start | bytes 393220
  0.6 25.4 %all-to-all-start = ((bf16[4,8,1024]{2,1,0:T(8,128)(2,1)}), bf16[4,8,1024]{2,1,0:T(8,128)(2,1)S(1)}, u32[]{:S(2)}, u32[]{:S(2)}) async-start(bf16[4,8,1024]{2,1,0:T(8,128)(2,1)} %param.6), calls=%async_computation | async-start | bytes 131072 | tf_op jit(solution)/shard_map/all_to_all | solution.py:100
  15.3 2.2 %copy-start = (bf16[2,1024,1024]{2,1,0:T(8,128)(2,1)S(1)}, bf16[2,1024,1024]{2,1,0:T(8,128)(2,1)}, u32[]{:S(2)}) copy-start(bf16[2,1024,1024]{2,1,0:T(8,128)(2,1)} %right_ref.1) | copy-start | bytes 12582916
  17.5 0.9 %copy-start.1 = (bf16[32,2048]{1,0:T(8,128)(2,1)S(1)}, bf16[32,2048]{1,0:T(8,128)(2,1)}, u32[]{:S(2)}) copy-start(bf16[32,2048]{1,0:T(8,128)(2,1)} %grad_ref.1) | copy-start | bytes 393220
  18.4 16.0 %copy-start.3 = (f32[32,2048]{1,0:T(8,128)S(1)}, f32[32,2048]{1,0:T(8,128)}, u32[]{:S(2)}) copy-start(f32[32,2048]{1,0:T(8,128)} %param.5) | copy-start | bytes 786436
  26.9 19.1 %all-to-all-start.1 = ((bf16[8,96,256]{2,1,0:T(8,128)(2,1)}), bf16[8,96,256]{2,1,0:T(8,128)(2,1)S(1)}, u32[]{:S(2)}, u32[]{:S(2)}) async-start(bf16[8,96,256]{2,1,0:T(8,128)(2,1)} %pack.1), calls=%async_computation.1 | async-start | bytes 786432 | tf_op jit(solution)/shard_map/all_to_all | solution.py:134
  46.8 12.4 %all-to-all-start.2 = ((bf16[4,8,32,256]{3,2,1,0:T(8,128)(2,1)}), bf16[4,8,32,256]{3,2,1,0:T(8,128)(2,1)S(1)}, u32[]{:S(2)}, u32[]{:S(2)}) async-start(bf16[4,8,32,256]{3,2,1,0:T(8,128)(2,1)} %broadcast_in_dim.10), calls=%async_computation.2 | async-start | bytes 1048576 | tf_op jit(solution)/shard_map/all_to_all | solution.py:137

commit v6 on v5

--- a/solution.py
+++ b/solution.py
@@ -1,3 +1,5 @@
+import functools
+
 import jax
 import jax.numpy as jnp
 from jax import lax
@@ -30,11 +32,36 @@
     return out
 
 
-def right_kernel(grad_ref, right_ref, out_ref):
+def right_kernel(
+    col_blocks, grad_ref, right_ref, part_ref, moment_ref, out_ref, next_ref, sums_ref, held_ref
+):
+    step = pl.program_id(0)
+    steps = pl.num_programs(0)
     both = jnp.dot(grad_ref[...], right_ref[0], preferred_element_type=F32).astype(BF16)
     cols = out_ref.shape[2]
     for i in range(both.shape[1] // cols):
         out_ref[i] = both[:, i * cols : (i + 1) * cols]
+    wide = part_ref[...].astype(F32)
+    moment_next = 0.95 * moment_ref[...] + 0.05 * wide * wide
+    next_ref[...] = moment_next
+    adam = wide / (jnp.sqrt(moment_next) + 1e-08)
+    square = jnp.sum(jnp.sum(adam * adam, axis=0, keepdims=True), axis=1, keepdims=True)
+    held_ref[step] = jnp.broadcast_to(square, held_ref.shape[1:])
+
+    @pl.when(step == steps - 1)
+    def _():
+        count = held_ref.shape[0] // col_blocks
+        values = []
+        for c in range(col_blocks):
+            total = held_ref[c * count]
+            for i in range(1, count):
+                total = total + held_ref[c * count + i]
+            values += split3(total)
+        lane = lax.broadcasted_iota(jnp.int32, sums_ref.shape, 1)
+        out = jnp.zeros(sums_ref.shape, F32)
+        for i, value in enumerate(values):
+            out = jnp.where(lane == 3 + i, value, out)
+        sums_ref[...] = out
 
 
 def pack_kernel(core_ref, piece_ref, left_ref, out_ref):
@@ -100,28 +127,31 @@
     mine = lax.all_to_all(left_roots, "zh", 0, 0, tiled=True)
     wide_cols = width // 4
     per_block = blk // wide_cols
-    pieces = pl.pallas_call(
-        right_kernel,
+    tile = lambda s: (0, s)
+    pieces, moment_next, adam_sums = pl.pallas_call(
+        functools.partial(right_kernel, col_blocks),
         grid=(4,),
-        out_shape=jax.ShapeDtypeStruct((YY, rows, cols), BF16),
+        out_shape=(
+            jax.ShapeDtypeStruct((YY, rows, cols), BF16),
+            jax.ShapeDtypeStruct((rows, width), F32),
+            jax.ShapeDtypeStruct((1, LANES), F32),
+        ),
         in_specs=[
             pl.BlockSpec((rows, blk), lambda s: (0, s // per_block)),
             pl.BlockSpec((1, blk, wide_cols), lambda s: (s // per_block, 0, s % per_block)),
+            pl.BlockSpec((rows, wide_cols), tile),
+            pl.BlockSpec((rows, wide_cols), tile),
         ],
-        out_specs=pl.BlockSpec((YY // 4, rows, cols), lambda s: (s, 0, 0)),
+        out_specs=(
+            pl.BlockSpec((YY // 4, rows, cols), lambda s: (s, 0, 0)),
+            pl.BlockSpec((rows, wide_cols), tile),
+            pl.BlockSpec((1, LANES), lambda s: (0, 0)),
+        ),
+        scratch_shapes=[pltpu.VMEM((4, 1, LANES), F32)],
         name="right",
         compiler_params=SMALL,
-        cost_estimate=pl.CostEstimate(flops=2**27, bytes_accessed=2**22, transcendentals=0),
-    )(grad, right_roots)
-    wide = grad.astype(F32)
-    moment_next = 0.95 * second_moment + 0.05 * wide * wide
-    adam = wide / (jnp.sqrt(moment_next) + 1e-08)
-    adam_part = jnp.sum((adam * adam).reshape(rows, col_blocks, blk), axis=(0, 2))
-    high = lax.reduce_precision(adam_part, 8, 7)
-    middle = lax.reduce_precision(adam_part - high, 8, 7)
-    adam_sums = jnp.stack([high, middle, adam_part - high - middle], axis=1).reshape(1, -1)
-    adam_sums = jnp.pad(adam_sums, ((0, 0), (3, LANES - 3 - adam_sums.shape[1])))
-
+        cost_estimate=pl.CostEstimate(flops=2**27, bytes_accessed=2**22, transcendentals=2**16),
+    )(grad, right_roots, grad, second_moment)
     send = pl.pallas_call(
         pack_kernel,
         out_shape=jax.ShapeDtypeStruct((YY, rows + ZH * sub * blk // (2 * cols), cols), BF16),
@@ -146,7 +176,7 @@
     )(strip, left, adam_sums)
     back = lax.all_to_all(ready, PLANE, 0, 0, tiled=True)
     update = pl.pallas_call(
-        lambda *refs: update_kernel(col_blocks, *refs),
+        functools.partial(update_kernel, col_blocks),
         out_shape=jax.ShapeDtypeStruct((rows, width), BF16),
         in_specs=[WHOLE],
         out_specs=WHOLE,

time: 75.2 us -> 74.1 us (0.985)
  blocking collectives: 16.6 us -> 35.5 us
  waiting for transfers between devices: 22.4 us -> 10.2 us
  starting transfers between devices: 26.5 us -> 18.8 us
  other arithmetic: 0.99 us -> 0 us
    all_to_all x0 -> x1, blocking collectives: none -> 18.9 us  [on_device(): got = lax.all_to_all(send, 'y', 0, 0, tiled=True)]
    all_to_all x1 -> x0, waiting for transfers between devices: 10.6 us -> none  [on_device(): got = lax.all_to_all(send, 'y', 0, 0, tiled=True)]
    all_to_all x1 -> x0, starting transfers between devices: 7.55 us -> none  [on_device(): got = lax.all_to_all(send, 'y', 0, 0, tiled=True)]
    all_to_all x1, waiting for transfers between devices: 6.24 us -> 4.32 us  [on_device(): mine = lax.all_to_all(left_roots, 'zh', 0, 0, tiled=True)]
    reduce_sum x2 -> x0, other arithmetic: 0.97 us -> none  [on_device(): jnp.sum((adam * adam).reshape(rows, col_blocks, blk), axis=(0, 2))]
    pallas_call x2, Pallas kernels: 2.23 us -> 3.2 us  [the longest x1 2.42 us: on_device(): pl.pallas_call(functools.partial(right_kernel, col_blocks), grid=(4,), ou...]
    unnamed x8 -> x6, local copies, waits for them, and re-layouts: 3.1 us -> 4.04 us
    pallas_call x1, Pallas kernels: 0.79 us -> 0.03 us  [on_device(): pl.pallas_call(pack_kernel, out_shape=jax.ShapeDtypeStruct((YY, rows + ZH...]
  transfers between devices with their start and end apart: 3 -> 2, of which waited for: 3 -> 2; matrix products, arithmetic and copies ran while one was open for 2% -> 0% of each run, Pallas kernels for 2% -> 3%
where the time goes in v6:
time: 74.1 us; the launch traced here: 73.7 us
  blocking collectives  35.5 us (48%)
  starting transfers between devices  18.8 us (25%)
  waiting for transfers between devices  10.2 us (14%)
  local copies, waits for them, and re-layouts  4.92 us (7%)
  Pallas kernels  3.63 us (5%)
    all_to_all x1, blocking collectives, on_device(): got = lax.all_to_all(send, 'y', 0, 0, tiled=True)  18.9 us
    all_to_all x1, starting transfers between devices, on_device(): mine = lax.all_to_all(left_roots, 'zh', 0, 0, tiled=True)  14.5 us
    all_to_all x1, blocking collectives, on_device(): back = lax.all_to_all(ready, PLANE, 0, 0, tiled=True)  14.4 us
    all_to_all x1, waiting for transfers between devices, on_device(): strip = lax.all_to_all(strip, 'x', 0, 0, tiled=True)  5.88 us
    all_to_all x1, waiting for transfers between devices, on_device(): mine = lax.all_to_all(left_roots, 'zh', 0, 0, tiled=True)  4.32 us
    all_to_all x1, starting transfers between devices, on_device(): strip = lax.all_to_all(strip, 'x', 0, 0, tiled=True)  4.29 us
    unnamed x6, local copies, waits for them, and re-layouts  4.04 us
    pallas_call x1, Pallas kernels, on_device(): pl.pallas_call(functools.partial(right_kernel, col_blocks), grid=(4,), ou...  2.42 us
  transfers between devices with their start and end apart: 2, of which 2 were waited for; matrix products, arithmetic and copies ran while one was open for 0% of the time, Pallas kernels for 3%

profile of v6, /device:TPU:8, one launch (start us, length us, event | category | flops | bytes accessed | tf_op | source)
XLA Modules:
  0.0 73.7 jit_solution(12229809721269257648)
XLA Ops:
  0.6 14.5 %all-to-all-start = ((bf16[4,8,1024]{2,1,0:T(8,128)(2,1)}), bf16[4,8,1024]{2,1,0:T(8,128)(2,1)S(1)}, u32[]{:S(2)}, u32[]{:S(2)}) async-start(bf16[4,8,1024]{2,1,0:T(8,128)(2,1)} %param.6), calls=%async_computation | async-start | bytes 131072 | tf_op jit(solution)/shard_map/all_to_all | solution.py:127
  15.1 0.0 copy-start
  15.1 2.2 %copy-done = bf16[2,1024,1024]{2,1,0:T(8,128)(2,1)S(1)} copy-done((bf16[2,1024,1024]{2,1,0:T(8,128)(2,1)S(1)}, bf16[2,1024,1024]{2,1,0:T(8,128)(2,1)}, u32[]{:S(2)}) %copy-start) | copy-done | bytes 4194328
  17.3 0.0 copy-start.1
  17.3 0.9 %copy-done.1 = bf16[32,2048]{1,0:T(8,128)(2,1)S(1)} copy-done((bf16[32,2048]{1,0:T(8,128)(2,1)S(1)}, bf16[32,2048]{1,0:T(8,128)(2,1)}, u32[]{:S(2)}) %copy-start.1) | copy-done | bytes 131096
  18.2 0.0 copy-start.2
  18.2 0.9 %copy-done.2 = f32[32,2048]{1,0:T(8,128)S(1)} copy-done((f32[32,2048]{1,0:T(8,128)S(1)}, f32[32,2048]{1,0:T(8,128)}, u32[]{:S(2)}) %copy-start.2) | copy-done | bytes 262168
  19.2 2.4 %right.1 = (bf16[8,32,256]{2,1,0:T(8,128)(2,1)S(1)}, f32[32,2048]{1,0:T(8,128)}, f32[1,128]{1,0:T(1,128)S(1)}) custom-call(bf16[32,2048]{1,0:T(8,128)(2,1)S(1)} %copy-done.1, bf16[2,1024,1024]{2,1,0:T(8,128)(2,1)S(1)} %copy-done, bf16[32,2048]{1,0:T(8,128)(2,1)S(1)} %copy-done.1, f32[32,2048]{1,0:T(8,128)S(1)} %copy-done.2), custom_call_target="tpu_custom_call" | custom-call | flops 134217728 | bytes 4194304 | tf_op jit(solution)/shard_map/right/pallas_call | solution.py:131
  21.6 4.3 %all-to-all-done.left_ref = bf16[4,8,1024]{2,1,0:T(8,128)(2,1)S(1)} async-done(((bf16[4,8,1024]{2,1,0:T(8,128)(2,1)}), bf16[4,8,1024]{2,1,0:T(8,128)(2,1)S(1)}, u32[]{:S(2)}, u32[]{:S(2)}) %all-to-all-start) | async-done | bytes 65568 | tf_op jit(solution)/shard_map/all_to_all | solution.py:127
  26.0 18.9 %all_to_all.20 = bf16[8,96,256]{2,1,0:T(8,128)(2,1)S(1)} all-to-all(bf16[8,96,256]{2,1,0:T(8,128)(2,1)S(1)} %pack.1), channel_id=1, replica_groups=mesh['zh'=4,'y'=8,'x'=4,'zl'=3,'core'=2] {'y'}, dimensions={0} | all-to-all | bytes 786432 | tf_op jit(solution)/shard_map/all_to_all | solution.py:164
  44.9 0.9 %broadcast_in_dim.10 = bf16[4,8,32,256]{3,2,1,0:T(8,128)(2,1)} broadcast(bf16[8,32,256]{2,1,0:T(8,128)(2,1)S(1)} %slice.8), dimensions={1,2,3} | broadcast | bytes 655360 | tf_op jit(solution)/shard_map/broadcast_in_dim | solution.py:166
  45.8 4.3 %all-to-all-start.2 = ((bf16[4,8,32,256]{3,2,1,0:T(8,128)(2,1)}), bf16[4,8,32,256]{3,2,1,0:T(8,128)(2,1)S(1)}, u32[]{:S(2)}, u32[]{:S(2)}) async-start(bf16[4,8,32,256]{3,2,1,0:T(8,128)(2,1)} %broadcast_in_dim.10), calls=%async_computation.2 | async-start | bytes 1048576 | tf_op jit(solution)/shard_map/all_to_all | solution.py:167
  50.1 2.2 %all-gather = bf16[16,64,256]{2,1,0:T(8,128)(2,1)S(1)} all-gather(bf16[8,64,256]{2,1,0:T(8,128)(2,1)S(1)} %slice.9), channel_id=2, replica_groups=mesh['zh'=4,'y'=8,'x'=4,'zl'=3,'core'=2] {'core'}, dimensions={0}, use_global_device_ids=true | all-gather | bytes 786432 | tf_op jit(solution)/shard_map/all_gather | solution.py:165
  52.3 5.9 %all-to-all-done.2.strip_ref = bf16[4,8,32,256]{3,2,1,0:T(8,128)(2,1)S(1)} async-done(((bf16[4,8,32,256]{3,2,1,0:T(8,128)(2,1)}), bf16[4,8,32,256]{3,2,1,0:T(8,128)(2,1)S(1)}, u32[]{:S(2)}, u32[]{:S(2)}) %all-to-all-start.2) | async-done | bytes 524320 | tf_op jit(solution)/shard_map/all_to_all | solution.py:167
  58.1 0.4 product.1
  58.6 14.4 %all_to_all.21.back_ref = bf16[32,8,384]{2,1,0:T(8,128)(2,1)S(1)} all-to-all(bf16[32,8,384]{2,1,0:T(8,128)(2,1)S(1)} %product.1), channel_id=1, replica_groups=mesh['zh'=4,'y'=8,'x'=4,'zl'=3,'core'=2] {'y','x'}, dimensions={0} | all-to-all | bytes 393216 | tf_op jit(solution)/shard_map/all_to_all | solution.py:177
  72.9 0.8 %update.1 = bf16[32,2048]{1,0:T(8,128)(2,1)} custom-call(bf16[32,8,384]{2,1,0:T(8,128)(2,1)S(1)} %all_to_all.21.back_ref), custom_call_target="tpu_custom_call" | custom-call | flops 4194304 | bytes 524288 | tf_op jit(solution)/shard_map/update/pallas_call | solution.py:178
  (3 shorter events, 0.1 us)
Async XLA Ops:
  0.6 25.3 %all-to-all-start = ((bf16[4,8,1024]{2,1,0:T(8,128)(2,1)}), bf16[4,8,1024]{2,1,0:T(8,128)(2,1)S(1)}, u32[]{:S(2)}, u32[]{:S(2)}) async-start(bf16[4,8,1024]{2,1,0:T(8,128)(2,1)} %param.6), calls=%async_computation | async-start | bytes 131072 | tf_op jit(solution)/shard_map/all_to_all | solution.py:127
  15.1 2.2 %copy-start = (bf16[2,1024,1024]{2,1,0:T(8,128)(2,1)S(1)}, bf16[2,1024,1024]{2,1,0:T(8,128)(2,1)}, u32[]{:S(2)}) copy-start(bf16[2,1024,1024]{2,1,0:T(8,128)(2,1)} %right_ref.1) | copy-start | bytes 12582916
  17.3 0.9 %copy-start.1 = (bf16[32,2048]{1,0:T(8,128)(2,1)S(1)}, bf16[32,2048]{1,0:T(8,128)(2,1)}, u32[]{:S(2)}) copy-start(bf16[32,2048]{1,0:T(8,128)(2,1)} %part_ref.1) | copy-start | bytes 393220
  18.2 0.9 %copy-start.2 = (f32[32,2048]{1,0:T(8,128)S(1)}, f32[32,2048]{1,0:T(8,128)}, u32[]{:S(2)}) copy-start(f32[32,2048]{1,0:T(8,128)} %moment_ref.1) | copy-start | bytes 786436
  45.8 12.4 %all-to-all-start.2 = ((bf16[4,8,32,256]{3,2,1,0:T(8,128)(2,1)}), bf16[4,8,32,256]{3,2,1,0:T(8,128)(2,1)S(1)}, u32[]{:S(2)}, u32[]{:S(2)}) async-start(bf16[4,8,32,256]{3,2,1,0:T(8,128)(2,1)} %broadcast_in_dim.10), calls=%async_computation.2 | async-start | bytes 1048576 | tf_op jit(solution)/shard_map/all_to_all | solution.py:167

commit v7 on v6

--- a/solution.py
+++ b/solution.py
@@ -64,12 +64,24 @@
         sums_ref[...] = out
 
 
+def reverse_kernel(left_ref, out_ref, sems):
+    copies = [
+        pltpu.make_async_copy(left_ref.at[z], out_ref.at[ZH - 1 - z], sems.at[z])
+        for z in range(ZH)
+    ]
+    for copy in copies:
+        copy.start()
+    for copy in copies:
+        copy.wait()
+
+
 def pack_kernel(core_ref, piece_ref, left_ref, out_ref):
     rows, cols = piece_ref.shape[1:]
     planes, sub, blk = left_ref.shape
     n = planes * sub
     half = blk // 2
-    left = left_ref[...].reshape(n, blk)
+    left = jnp.concatenate([left_ref[ZH - 1 - z].astype(F32) for z in range(ZH)], axis=0)
+    left = left.astype(BF16)
     left = jnp.where(core_ref[0] == 0, left[:, :half], left[:, half:])
     for j in range(YY):
         out_ref[j, :rows] = piece_ref[j]
@@ -124,7 +136,16 @@
     col_blocks, blk = right_roots.shape[:2]
     cols = width // YY
     sub = rows // XX
-    mine = lax.all_to_all(left_roots, "zh", 0, 0, tiled=True)
+    backward = pl.pallas_call(
+        reverse_kernel,
+        out_shape=jax.ShapeDtypeStruct(left_roots.shape, BF16),
+        in_specs=[pl.BlockSpec(memory_space=pl.ANY)],
+        out_specs=pl.BlockSpec(memory_space=pl.ANY),
+        scratch_shapes=[pltpu.SemaphoreType.DMA((ZH,))],
+        name="reverse",
+    )(left_roots)
+    turned = [list(range(ZH))[::-1]]
+    mine = lax.all_to_all(backward, "zh", 0, 0, axis_index_groups=turned, tiled=True)
     wide_cols = width // 4
     per_block = blk // wide_cols
     tile = lambda s: (0, s)

time: 74.1 us -> 76 us (1.026)
  waiting for transfers between devices: 10.2 us -> 5.98 us
  Pallas kernels: 3.63 us -> 6.76 us
  blocking collectives: 35.5 us -> 37.1 us
  starting transfers between devices: 18.8 us -> 20.2 us
    all_to_all x1, waiting for transfers between devices: 4.32 us -> 0.1 us  [on_device(): lax.all_to_all(backward, 'zh', 0, 0, axis_index_groups=turned, tiled=True)]
    pallas_call x0 -> x1, Pallas kernels: none -> 3.12 us  [on_device(): pl.pallas_call(reverse_kernel, out_shape=jax.ShapeDtypeStruct(left_roots....]
    all_to_all x1, starting transfers between devices: 14.5 us -> 15.9 us  [on_device(): lax.all_to_all(backward, 'zh', 0, 0, axis_index_groups=turned, tiled=True)]
    all_to_all x1, blocking collectives: 18.9 us -> 20.2 us  [on_device(): got = lax.all_to_all(send, 'y', 0, 0, tiled=True)]
where the time goes in v7:
time: 76 us; the launch traced here: 75.6 us
  blocking collectives  37.1 us (49%)
  starting transfers between devices  20.2 us (27%)
  Pallas kernels  6.76 us (9%)
  waiting for transfers between devices  5.98 us (8%)
  local copies, waits for them, and re-layouts  4.92 us (6%)
    all_to_all x1, blocking collectives, on_device(): got = lax.all_to_all(send, 'y', 0, 0, tiled=True)  20.2 us
    all_to_all x1, starting transfers between devices, on_device(): lax.all_to_all(backward, 'zh', 0, 0, axis_index_groups=turned, tiled=True)  15.9 us
    all_to_all x1, blocking collectives, on_device(): back = lax.all_to_all(ready, PLANE, 0, 0, tiled=True)  14.7 us
    all_to_all x1, waiting for transfers between devices, on_device(): strip = lax.all_to_all(strip, 'x', 0, 0, tiled=True)  5.88 us
    all_to_all x1, starting transfers between devices, on_device(): strip = lax.all_to_all(strip, 'x', 0, 0, tiled=True)  4.29 us
    unnamed x6, local copies, waits for them, and re-layouts  4.04 us
    pallas_call x1, Pallas kernels, on_device(): pl.pallas_call(reverse_kernel, out_shape=jax.ShapeDtypeStruct(left_roots....  3.12 us
    pallas_call x1, Pallas kernels, on_device(): pl.pallas_call(functools.partial(right_kernel, col_blocks), grid=(4,), ou...  2.42 us
  transfers between devices with their start and end apart: 2, of which 2 were waited for; matrix products, arithmetic and copies ran while one was open for 0% of the time, Pallas kernels for 3%

profile of v7, /device:TPU:8, one launch (start us, length us, event | category | flops | bytes accessed | tf_op | source)
XLA Modules:
  0.0 75.6 jit_solution(11856370813974935236)
XLA Ops:
  0.6 3.1 %reverse.1 = bf16[4,8,1024]{2,1,0:T(8,128)(2,1)} custom-call(bf16[4,8,1024]{2,1,0:T(8,128)(2,1)} %left_ref.1), custom_call_target="tpu_custom_call" | custom-call | tf_op jit(solution)/shard_map/reverse/pallas_call | solution.py:139
  3.8 15.9 %all-to-all-start = ((bf16[4,8,1024]{2,1,0:T(8,128)(2,1)}), bf16[4,8,1024]{2,1,0:T(8,128)(2,1)S(1)}, u32[]{:S(2)}, u32[]{:S(2)}) async-start(bf16[4,8,1024]{2,1,0:T(8,128)(2,1)} %reverse.1), calls=%async_computation | async-start | bytes 131072 | tf_op jit(solution)/shard_map/all_to_all | solution.py:148
  19.7 0.0 copy-start
  19.7 2.2 %copy-done = bf16[2,1024,1024]{2,1,0:T(8,128)(2,1)S(1)} copy-done((bf16[2,1024,1024]{2,1,0:T(8,128)(2,1)S(1)}, bf16[2,1024,1024]{2,1,0:T(8,128)(2,1)}, u32[]{:S(2)}) %copy-start) | copy-done | bytes 4194328
  21.9 0.0 copy-start.1
  21.9 0.9 %copy-done.1 = bf16[32,2048]{1,0:T(8,128)(2,1)S(1)} copy-done((bf16[32,2048]{1,0:T(8,128)(2,1)S(1)}, bf16[32,2048]{1,0:T(8,128)(2,1)}, u32[]{:S(2)}) %copy-start.1) | copy-done | bytes 131096
  22.8 0.0 copy-start.2
  22.8 0.9 %copy-done.2 = f32[32,2048]{1,0:T(8,128)S(1)} copy-done((f32[32,2048]{1,0:T(8,128)S(1)}, f32[32,2048]{1,0:T(8,128)}, u32[]{:S(2)}) %copy-start.2) | copy-done | bytes 262168
  23.7 2.4 %right.1 = (bf16[8,32,256]{2,1,0:T(8,128)(2,1)S(1)}, f32[32,2048]{1,0:T(8,128)}, f32[1,128]{1,0:T(1,128)S(1)}) custom-call(bf16[32,2048]{1,0:T(8,128)(2,1)S(1)} %copy-done.1, bf16[2,1024,1024]{2,1,0:T(8,128)(2,1)S(1)} %copy-done, bf16[32,2048]{1,0:T(8,128)(2,1)S(1)} %copy-done.1, f32[32,2048]{1,0:T(8,128)S(1)} %copy-done.2), custom_call_target="tpu_custom_call" | custom-call | flops 134217728 | bytes 4194304 | tf_op jit(solution)/shard_map/right/pallas_call | solution.py:152
  26.1 0.1 all-to-all-done.left_ref
  26.3 20.2 %all_to_all.20 = bf16[8,96,256]{2,1,0:T(8,128)(2,1)S(1)} all-to-all(bf16[8,96,256]{2,1,0:T(8,128)(2,1)S(1)} %pack.1), channel_id=1, replica_groups=mesh['zh'=4,'y'=8,'x'=4,'zl'=3,'core'=2] {'y'}, dimensions={0} | all-to-all | bytes 786432 | tf_op jit(solution)/shard_map/all_to_all | solution.py:185
  46.5 0.9 %broadcast_in_dim.10 = bf16[4,8,32,256]{3,2,1,0:T(8,128)(2,1)} broadcast(bf16[8,32,256]{2,1,0:T(8,128)(2,1)S(1)} %slice.8), dimensions={1,2,3} | broadcast | bytes 655360 | tf_op jit(solution)/shard_map/broadcast_in_dim | solution.py:187
  47.3 4.3 %all-to-all-start.2 = ((bf16[4,8,32,256]{3,2,1,0:T(8,128)(2,1)}), bf16[4,8,32,256]{3,2,1,0:T(8,128)(2,1)S(1)}, u32[]{:S(2)}, u32[]{:S(2)}) async-start(bf16[4,8,32,256]{3,2,1,0:T(8,128)(2,1)} %broadcast_in_dim.10), calls=%async_computation.2 | async-start | bytes 1048576 | tf_op jit(solution)/shard_map/all_to_all | solution.py:188
  51.7 2.2 %all-gather = bf16[16,64,256]{2,1,0:T(8,128)(2,1)S(1)} all-gather(bf16[8,64,256]{2,1,0:T(8,128)(2,1)S(1)} %slice.9), channel_id=2, replica_groups=mesh['zh'=4,'y'=8,'x'=4,'zl'=3,'core'=2] {'core'}, dimensions={0}, use_global_device_ids=true | all-gather | bytes 786432 | tf_op jit(solution)/shard_map/all_gather | solution.py:186
  53.8 5.9 %all-to-all-done.2.strip_ref = bf16[4,8,32,256]{3,2,1,0:T(8,128)(2,1)S(1)} async-done(((bf16[4,8,32,256]{3,2,1,0:T(8,128)(2,1)}), bf16[4,8,32,256]{3,2,1,0:T(8,128)(2,1)S(1)}, u32[]{:S(2)}, u32[]{:S(2)}) %all-to-all-start.2) | async-done | bytes 524320 | tf_op jit(solution)/shard_map/all_to_all | solution.py:188
  59.7 0.4 product.1
  60.1 14.7 %all_to_all.21.back_ref = bf16[32,8,384]{2,1,0:T(8,128)(2,1)S(1)} all-to-all(bf16[32,8,384]{2,1,0:T(8,128)(2,1)S(1)} %product.1), channel_id=1, replica_groups=mesh['zh'=4,'y'=8,'x'=4,'zl'=3,'core'=2] {'y','x'}, dimensions={0} | all-to-all | bytes 393216 | tf_op jit(solution)/shard_map/all_to_all | solution.py:198
  74.8 0.8 %update.1 = bf16[32,2048]{1,0:T(8,128)(2,1)} custom-call(bf16[32,8,384]{2,1,0:T(8,128)(2,1)S(1)} %all_to_all.21.back_ref), custom_call_target="tpu_custom_call" | custom-call | flops 4194304 | bytes 524288 | tf_op jit(solution)/shard_map/update/pallas_call | solution.py:199
  (3 shorter events, 0.1 us)
Async XLA Ops:
  3.8 22.5 %all-to-all-start = ((bf16[4,8,1024]{2,1,0:T(8,128)(2,1)}), bf16[4,8,1024]{2,1,0:T(8,128)(2,1)S(1)}, u32[]{:S(2)}, u32[]{:S(2)}) async-start(bf16[4,8,1024]{2,1,0:T(8,128)(2,1)} %reverse.1), calls=%async_computation | async-start | bytes 131072 | tf_op jit(solution)/shard_map/all_to_all | solution.py:148
  19.7 2.2 %copy-start = (bf16[2,1024,1024]{2,1,0:T(8,128)(2,1)S(1)}, bf16[2,1024,1024]{2,1,0:T(8,128)(2,1)}, u32[]{:S(2)}) copy-start(bf16[2,1024,1024]{2,1,0:T(8,128)(2,1)} %right_ref.1) | copy-start | bytes 12582916
  21.9 0.9 %copy-start.1 = (bf16[32,2048]{1,0:T(8,128)(2,1)S(1)}, bf16[32,2048]{1,0:T(8,128)(2,1)}, u32[]{:S(2)}) copy-start(bf16[32,2048]{1,0:T(8,128)(2,1)} %part_ref.1) | copy-start | bytes 393220
  22.8 0.9 %copy-start.2 = (f32[32,2048]{1,0:T(8,128)S(1)}, f32[32,2048]{1,0:T(8,128)}, u32[]{:S(2)}) copy-start(f32[32,2048]{1,0:T(8,128)} %moment_ref.1) | copy-start | bytes 786436
  47.3 12.4 %all-to-all-start.2 = ((bf16[4,8,32,256]{3,2,1,0:T(8,128)(2,1)}), bf16[4,8,32,256]{3,2,1,0:T(8,128)(2,1)S(1)}, u32[]{:S(2)}, u32[]{:S(2)}) async-start(bf16[4,8,32,256]{3,2,1,0:T(8,128)(2,1)} %broadcast_in_dim.10), calls=%async_computation.2 | async-start | bytes 1048576 | tf_op jit(solution)/shard_map/all_to_all | solution.py:188
